TPU v7x, 128 devices: a whole 4x4x4 slice. The times are simulated.
128 devices in a mesh: leaf: 8 (over x, core), front: 16 (over y, z).
Axes of the slice: x: 4, y: 4, z: 4, core: 2. Of those that a mesh axis runs over, the one named last changes fastest.
Arguments:
- tiles: bfloat16 [2, 8, 16, 24, 128, 128], P(None, 'leaf', 'front'), may hold values from -2304 to 2304, as said below
- tile_pos: int32 [2, 8, 16, 2, 24], P(None, 'leaf'), may hold values from 0 to 31, as said below
- diag: float32 [2, 8, 4096], P(None, 'leaf', 'front'), may hold values from 0.2 to 1
- parent_blocks: int32 [8, 13], P('leaf'), may hold values from 0 to 15, as said below
Outputs:
- leaf_fronts: float32 [8, 4096, 4096], P('leaf', None, 'front')
- merged_fronts: float32 [8, 4096, 4096], P('leaf', None, 'front')
Inputs may be any that keep to these rules, and one draw needn't show every extreme that they name: `tiles`: together with diag, every orig[l,g] is symmetric positive definite. `tile_pos`: every tile's row index is at least its column index. On one device and level, counting both indices of each tile (a diagonal tile twice), every tile index occurs either not at all or exactly 3 times; one index, the same on every device and level, occurs on every device. `parent_blocks`: each row is strictly increasing, begins with 0 and ends with 15.
All inputs are finite; a program needn't handle non-finite values.
Results may differ from a plain program's by a relative error of at most 0.0003.
Values may be sent and summed in bfloat16 or wider, within the bound.
A program may use at most 192 MiB of HBM per device.

v0:
```python
import jax
import jax.numpy as jnp
from jax import lax
from jax.sharding import PartitionSpec as P

F = 4096
B = 256
TB = 128
PANELS = 3
MOST = 3
PIV = 768
UB = 13
NBLK = 16
NTC = 32


def from_root(value, axis, source):
    kept = jnp.where(lax.axis_index(axis) == source, value, 0).astype(value.dtype)
    return lax.psum(kept, axis)


def from_partner(block, axis, stride):
    count = lax.axis_size(axis)
    route = []
    for low in range(count):
        high = low | 1 << stride
        if high != low and high < count:
            route += [(low, high), (high, low)]
    return lax.ppermute(block, axis, route)


def factor_panel(column):
    diag_factor = jnp.linalg.cholesky(column[:B])
    below_factor = lax.linalg.triangular_solve(
        diag_factor, column[B:], left_side=False, lower=True, transpose_a=True
    )
    return jnp.concatenate([diag_factor, below_factor], axis=0)


def zeros_like_panel(column):
    return jnp.zeros_like(column)


def tile_items(positions):
    tile_rows = positions[0]
    tile_cols = positions[1]
    item_cols = jnp.concatenate([tile_cols, tile_rows])
    item_rows = jnp.concatenate([tile_rows, tile_cols])
    item_count = item_cols.shape[0]
    earlier = jnp.arange(item_count)[None, :] < jnp.arange(item_count)[:, None]
    same_column = item_cols[:, None] == item_cols[None, :]
    item_slots = jnp.sum(jnp.logical_and(same_column, earlier), axis=1)
    return (item_cols, item_rows, item_slots)


def assemble_local(level_tiles, positions, diag_here, front_index, col_width):
    front_count = positions.shape[0]
    own_positions = lax.dynamic_index_in_dim(positions, front_index, 0, keepdims=False)
    own_cols, own_rows, own_slots = tile_items(own_positions)
    tile_values = jnp.concatenate([level_tiles, jnp.swapaxes(level_tiles, 1, 2)], axis=0)
    outgoing = jnp.zeros((NTC, MOST, TB, TB), jnp.bfloat16).at[own_cols, own_slots].set(tile_values)
    incoming = lax.all_to_all(outgoing, "front", split_axis=0, concat_axis=1, tiled=True)
    all_cols, all_rows, all_slots = jax.vmap(tile_items)(positions)
    local_tiles = col_width // TB
    first_tile = front_index * local_tiles
    col_hot = (all_cols[:, :, None] == first_tile + jnp.arange(local_tiles)[None, None, :]).astype(
        jnp.float32
    )
    slot_hot = (all_slots[:, :, None] == jnp.arange(MOST)[None, None, :]).astype(jnp.float32)
    row_hot = (all_rows[:, :, None] == jnp.arange(NTC)[None, None, :]).astype(jnp.float32)
    placement = jnp.einsum(
        "sil,sim,sir->lsmr", col_hot, slot_hot, row_hot, precision=lax.Precision.HIGHEST
    ).astype(jnp.bfloat16)
    arranged = incoming.reshape(local_tiles, front_count, MOST, TB, TB)
    hessian = jnp.einsum(
        "lsmr,lsmab->ralb", placement, arranged, preferred_element_type=jnp.float32
    ).reshape(F, col_width)
    weight_scale = 1.0 / (MOST * front_count * TB)
    cols_global = front_index * col_width + jnp.arange(col_width)
    row_index = jnp.arange(F)
    diagonal = jnp.where(row_index[:, None] == cols_global[None, :], diag_here[None, :], 0.0)
    return weight_scale * hessian + diagonal


def extend_local(matrix, blocks, front_index):
    col_width = matrix.shape[1]
    cols_global = front_index * col_width + jnp.arange(col_width)
    block_hot = (blocks[:, None] == jnp.arange(NBLK)[None, :]).astype(jnp.float32)
    schur_cols = jnp.where((cols_global >= PIV)[None, :], matrix[PIV:, :], 0.0)
    as_rows = schur_cols.T.reshape(col_width, UB, B)
    spread = jnp.einsum("wub,up->wpb", as_rows, block_hot, precision=lax.Precision.HIGHEST)
    incoming = lax.all_to_all(spread, "front", split_axis=1, concat_axis=0, tiled=True)
    gathered = incoming.reshape(F, col_width)[PIV:].reshape(UB, B, col_width)
    placed = jnp.einsum("ubc,up->pbc", gathered, block_hot, precision=lax.Precision.HIGHEST)
    return placed.reshape(F, col_width)


def factor_panels(matrix, front_index, share_panel):
    col_width = matrix.shape[1]
    cols_global = front_index * col_width + jnp.arange(col_width)
    for step in range(PANELS):
        first_row = step * B
        owner_rank = first_row // col_width
        offset = first_row - owner_rank * col_width
        column = matrix[first_row:, offset : offset + B]
        panel_tail = share_panel(column, owner_rank)
        panel_full = jnp.concatenate([jnp.zeros((first_row, B), jnp.float32), panel_tail], axis=0)
        matrix = jnp.where(
            front_index == owner_rank, matrix.at[:, offset : offset + B].set(panel_full), matrix
        )
        below_row = first_row + B
        rows_mine = lax.dynamic_slice_in_dim(panel_full, front_index * col_width, col_width, 0)
        rows_mine = jnp.where((cols_global >= below_row)[:, None], rows_mine, 0.0)
        matrix = matrix.at[below_row:, :].add(
            -jnp.dot(panel_full[below_row:], rows_mine.T, precision=lax.Precision.HIGHEST)
        )
    return matrix


def factor_front(matrix, front_index):

    def share_factored(column, owner_rank):
        factored = lax.cond(front_index == owner_rank, factor_panel, zeros_like_panel, column)
        return from_root(factored, "front", owner_rank)

    matrix = factor_panels(matrix, front_index, share_factored)
    return matrix


def body(tiles, tile_pos, diag, parent_blocks):
    front_index = lax.axis_index("front")
    col_width = diag.shape[2]
    cols_global = front_index * col_width + jnp.arange(col_width)
    row_index = jnp.arange(F)
    lower_mask = row_index[:, None] >= cols_global[None, :]
    leaf_front = assemble_local(tiles[0, 0, 0], tile_pos[0, 0], diag[0, 0], front_index, col_width)
    leaf_front = factor_front(leaf_front, front_index)
    own_part = assemble_local(tiles[1, 0, 0], tile_pos[1, 0], diag[1, 0], front_index, col_width)
    contribution = own_part + extend_local(leaf_front, parent_blocks[0], front_index)
    sibling = from_partner(contribution, "leaf", 0)
    merged = factor_front(contribution + sibling, front_index)
    leaf_out = jnp.where(lower_mask, leaf_front, 0.0)
    merged_out = jnp.where(lower_mask, merged, 0.0)
    return (leaf_out[None], merged_out[None])


def solution(mesh):
    placed = (
        P(None, "leaf", "front", None, None, None),
        P(None, "leaf", None, None, None),
        P(None, "leaf", "front"),
        P("leaf", None),
    )
    return jax.shard_map(
        body,
        mesh=mesh,
        in_specs=placed,
        out_specs=(P("leaf", None, "front"), P("leaf", None, "front")),
        check_vma=False,
    )
```

profile of v0, /device:TPU:9, one launch (start us, length us, event | category | flops | bytes accessed | tf_op | source)
XLA Modules:
  0.0 1445.1 jit_solution(16596002789575852275)
XLA Ops:
  15.9 7.1 scatter_fusion
  23.1 8.0 all-to-all-start
  34.4 35.5 %all-to-all-done = bf16[32,3,128,128]{3,2,1,0:T(8,128)(2,1)S(1)} async-done(((bf16[32,3,128,128]{3,2,1,0:T(8,128)(2,1)}), bf16[32,3,128,128]{3,2,1,0:T(8,128)(2,1)S(1)}, u32[]{:S(2)}, u32[]{:S(2)}) %all-to-all-start) | async-done | bytes 3145760 | tf_op jit(solution)/shard_map/all_to_all | solution.py:62
  78.7 5.4 conditional.6
  86.5 189.7 %all-reduce.12.cloned.1.call-done = f32[4096,256]{1,0:T(8,128)} async-done(((f32[4096,256]{1,0:T(8,128)}), f32[4096,256]{1,0:T(8,128)}) %all-reduce.12.cloned.1.call-update) | async-done | bytes 4194320 | tf_op jit(solution)/shard_map/psum | solution.py:19
  276.2 5.0 broadcast_select_fusion.3
  281.2 6.5 fusion.60
  287.7 5.3 conditional.7
  295.3 182.9 %all-reduce.14.cloned.1.call-done = f32[3840,256]{1,0:T(8,128)} async-done(((f32[3840,256]{1,0:T(8,128)}), f32[3840,256]{1,0:T(8,128)}) %all-reduce.14.cloned.1.call-update) | async-done | bytes 3932176 | tf_op jit(solution)/shard_map/psum | solution.py:19
  478.2 6.1 pad_select_fusion.3
  484.2 6.2 fusion.58
  490.4 10.7 conditional.8
  507.0 7.1 scatter_fusion.1
  514.2 83.8 %all-to-all-start.1 = ((bf16[32,3,128,128]{3,2,1,0:T(8,128)(2,1)}), bf16[32,3,128,128]{3,2,1,0:T(8,128)(2,1)}, u32[]{:S(2)}, u32[]{:S(2)}) async-start(bf16[32,3,128,128]{3,2,1,0:T(8,128)(2,1)} %scatter_fusion.1), calls=%async_computation.1 | async-start | bytes 6291456 | tf_op jit(solution)/shard_map/all_to_all | solution.py:62
  597.9 112.9 %all-reduce.16.cloned.1.call-done = f32[3584,256]{1,0:T(8,128)} async-done(((f32[3584,256]{1,0:T(8,128)}), f32[3584,256]{1,0:T(8,128)}) %all-reduce.16.cloned.1.call-update) | async-done | bytes 3670032 | tf_op jit(solution)/shard_map/psum | solution.py:19
  710.8 6.0 pad_select_fusion.1
  716.8 5.1 fusion.56
  736.2 5.4 all-to-all-start.2
  746.4 5.2 copy.181
  751.7 42.2 %all-to-all-done.2 = f32[256,16,256]{2,0,1:T(8,128)} async-done(((f32[256,16,256]{2,0,1:T(8,128)}), f32[256,16,256]{2,0,1:T(8,128)}, u32[]{:S(2)}, u32[]{:S(2)}) %all-to-all-start.2) | async-done | bytes 4194336 | tf_op jit(solution)/shard_map/all_to_all | solution.py:92
  807.9 6.8 collective-permute-done
  817.3 5.5 conditional.9
  825.1 193.5 %all-reduce.18.cloned.1.call-done = f32[4096,256]{1,0:T(8,128)} async-done(((f32[4096,256]{1,0:T(8,128)}), f32[4096,256]{1,0:T(8,128)}) %all-reduce.18.cloned.1.call-update) | async-done | bytes 4194320 | tf_op jit(solution)/shard_map/psum | solution.py:19
  1023.5 6.5 fusion.66
  1030.0 5.1 conditional.10
  1037.3 183.3 %all-reduce.20.cloned.1.call-done = f32[3840,256]{1,0:T(8,128)} async-done(((f32[3840,256]{1,0:T(8,128)}), f32[3840,256]{1,0:T(8,128)}) %all-reduce.20.cloned.1.call-update) | async-done | bytes 3932176 | tf_op jit(solution)/shard_map/psum | solution.py:19
  1220.6 6.1 pad_select_fusion.2
  1226.7 6.2 fusion.69
  1232.9 7.2 conditional.11
  1242.1 180.1 %all-reduce.22.cloned.1.call-done = f32[3584,256]{1,0:T(8,128)} async-done(((f32[3584,256]{1,0:T(8,128)}), f32[3584,256]{1,0:T(8,128)}) %all-reduce.22.cloned.1.call-update) | async-done | bytes 3670032 | tf_op jit(solution)/shard_map/psum | solution.py:19
  1426.6 4.9 fusion.55
  1431.5 6.3 select_bitcast_fusion.6
  (116 shorter events, 95.9 us)
Async XLA Ops:
  23.1 10.7 copy-start.18
  23.1 46.8 %all-to-all-start = ((bf16[32,3,128,128]{3,2,1,0:T(8,128)(2,1)}), bf16[32,3,128,128]{3,2,1,0:T(8,128)(2,1)S(1)}, u32[]{:S(2)}, u32[]{:S(2)}) async-start(bf16[32,3,128,128]{3,2,1,0:T(8,128)(2,1)} %scatter_fusion), calls=%async_computation | async-start | bytes 6291456 | tf_op jit(solution)/shard_map/all_to_all | solution.py:62
  31.1 245.1 %all-reduce.12.cloned.1.call-start = ((), (), s32[]{:S(2)}) async-start(), calls=%async_computation.3 | async-start | bytes 8388608 | tf_op jit(solution)/shard_map/psum | solution.py:19
  75.5 3.2 copy-start
  86.4 391.7 %all-reduce.14.cloned.1.call-start = ((), (), s32[]{:S(2)}) async-start(), calls=%async_computation.4 | async-start | bytes 7864320 | tf_op jit(solution)/shard_map/psum | solution.py:19
  86.5 194.7 %copy-start.14 = (pred[256]{0:T(512)(128)(4,1)}, pred[256]{0:T(512)(128)(4,1)S(1)}, u32[]{:S(2)}) copy-start(pred[256]{0:T(512)(128)(4,1)S(1)} %fusion.142) | copy-start | bytes 772
  276.2 5.0 copy-start.3
  295.2 415.7 %all-reduce.16.cloned.1.call-start = ((), (), s32[]{:S(2)}) async-start(), calls=%async_computation.5 | async-start | bytes 7340032 | tf_op jit(solution)/shard_map/psum | solution.py:19
  295.2 189.0 %copy-start.16 = (pred[256]{0:T(512)(128)(4,1)}, pred[256]{0:T(512)(128)(4,1)S(1)}, u32[]{:S(2)}) copy-start(pred[256]{0:T(512)(128)(4,1)S(1)} %fusion.141) | copy-start | bytes 772
  478.2 6.1 copy-start.4
  501.1 2.1 copy-start.8
  503.2 0.7 copy-start.20
  503.2 1.1 copy-start.9
  503.2 1.3 copy-start.19
  514.2 222.1 %all-to-all-start.1 = ((bf16[32,3,128,128]{3,2,1,0:T(8,128)(2,1)}), bf16[32,3,128,128]{3,2,1,0:T(8,128)(2,1)}, u32[]{:S(2)}, u32[]{:S(2)}) async-start(bf16[32,3,128,128]{3,2,1,0:T(8,128)(2,1)} %scatter_fusion.1), calls=%async_computation.1 | async-start | bytes 6291456 | tf_op jit(solution)/shard_map/all_to_all | solution.py:62
  710.8 6.0 copy-start.6
  724.2 3.4 copy-start.13
  736.2 5.6 copy-start.10
  736.2 5.6 copy-start.11
  736.2 57.7 %all-to-all-start.2 = ((f32[256,16,256]{2,0,1:T(8,128)}), f32[256,16,256]{2,0,1:T(8,128)}, u32[]{:S(2)}, u32[]{:S(2)}) async-start(f32[256,16,256]{2,0,1:T(8,128)} %copy.161), calls=%async_computation.2 | async-start | bytes 8388608 | tf_op jit(solution)/shard_map/all_to_all | solution.py:92
  741.6 277.0 %all-reduce.18.cloned.1.call-start = ((), (), s32[]{:S(2)}) async-start(), calls=%async_computation.6 | async-start | bytes 8388608 | tf_op jit(solution)/shard_map/psum | solution.py:19
  800.9 2.7 copy-start.1
  800.9 2.7 copy-start.12
  804.7 10.0 collective-permute-start
  825.0 395.6 %all-reduce.20.cloned.1.call-start = ((), (), s32[]{:S(2)}) async-start(), calls=%async_computation.7 | async-start | bytes 7864320 | tf_op jit(solution)/shard_map/psum | solution.py:19
  825.1 198.5 %copy-start.15 = (pred[256]{0:T(512)(128)(4,1)S(1)}, pred[256]{0:T(512)(128)(4,1)}, u32[]{:S(2)}) copy-start(pred[256]{0:T(512)(128)(4,1)} %copy-done.14) | copy-start | bytes 772
  1018.6 4.9 copy-start.2
  1037.2 385.0 %all-reduce.22.cloned.1.call-start = ((), (), s32[]{:S(2)}) async-start(), calls=%async_computation.8 | async-start | bytes 7340032 | tf_op jit(solution)/shard_map/psum | solution.py:19
  1037.3 189.4 %copy-start.17 = (pred[256]{0:T(512)(128)(4,1)S(1)}, pred[256]{0:T(512)(128)(4,1)}, u32[]{:S(2)}) copy-start(pred[256]{0:T(512)(128)(4,1)} %copy-done.16) | copy-start | bytes 772
  1220.6 6.1 copy-start.5
  1422.2 4.3 copy-start.7
Sparse Core Ops, SparseCore 0:
  86.6 189.5 all-reduce.11
  295.3 182.8 all-reduce.13
  503.4 207.4 all-reduce.15
  825.1 193.4 all-reduce.17
  1037.4 183.2 all-reduce.19
  1242.2 179.9 all-reduce.21
where the time goes:
time: 1460 us; the launch traced here: 1450 us
  waiting for transfers between devices  1130 us (77%)
  starting transfers between devices  101 us (7%)
  other arithmetic  64 us (4%)
  local copies, waits for them, and re-layouts  63.1 us (4%)
  matrix products  49.1 us (3%)
  loops' own time  26 us (2%)
  between operations  15 us (1%)
    psum x6, waiting for transfers between devices, from_root(): return lax.psum(kept, axis)  1040 us
    all_to_all x2, starting transfers between devices, assemble_local(): lax.all_to_all(outgoing, 'front', split_axis=0, concat_axis=1, tiled=True)  91.7 us
    all_to_all x1, waiting for transfers between devices, extend_local(): lax.all_to_all(spread, 'front', split_axis=1, concat_axis=0, tiled=True)  42.2 us
    all_to_all x2, waiting for transfers between devices, assemble_local(): lax.all_to_all(outgoing, 'front', split_axis=0, concat_axis=1, tiled=True)  35.5 us
    dot_general x6, matrix products, factor_panels(): jnp.dot(panel_full[below_row:], rows_mine.T, precision=lax.Precision.HIGH...  35.2 us
    select_n x6, other arithmetic, factor_panels(): jnp.where(front_index == owner_rank, matrix.at[:, offset:offset + B].set(...  32.1 us
  transfers between devices with their start and end apart: 10, of which 9 were waited for; matrix products, arithmetic and copies ran while one was open for 3% of the time, Pallas kernels for 0%

commit v1 on v0

v1 whole, which is shorter than its diff:
```python
import functools

import jax
import jax.numpy as jnp
from jax import lax
from jax.experimental import pallas as pl
from jax.experimental.pallas import tpu as pltpu
from jax.sharding import PartitionSpec as P

F = 4096
B = 256
TB = 128
PIV = 768
UB = 13
T = 24
NF = 16
SCALE = 1.0 / 6144.0
MESH = pl.DeviceIdType.MESH
HI = lax.Precision.HIGHEST
f32 = jnp.float32
bf16 = jnp.bfloat16
VM = pl.BlockSpec(memory_space=pltpu.VMEM)
SM = pl.BlockSpec(memory_space=pltpu.SMEM)
LIMIT = 56 << 20
WIDTH = 8


def params(**more):
    return pltpu.CompilerParams(vmem_limit_bytes=LIMIT, **more)


def f32s(*shape):
    return jax.ShapeDtypeStruct(shape, f32)


def dot(a, b, ca, cb):
    return lax.dot_general(
        a, b, (((ca,), (cb,)), ((), ())), precision=HI, preferred_element_type=f32
    )


def row_col(pos, level, src, t):
    base = (level * NF + src) * 2 * T
    return pos[base + t], pos[base + T + t]


def lifted(pb, index):
    return 2 * pb[jnp.maximum(index - 6, 0) // 2] + lax.rem(index, 2)


def owner(r, c):
    return jnp.where(c >= 6, c, r)


def pack_kernel(pos, pb, tiles, slab, big0, bigm, cnt):
    me = lax.axis_index("front")

    def clear(i, _):
        cnt[i] = 0
        return 0

    lax.fori_loop(0, 64, clear, 0)

    def bump(i):
        old = cnt[i]
        cnt[i] = old + 1
        return old

    def put_slab(value, par, slot):
        for h in range(8):
            slab[par * 8 + h, slot] = value[16 * h : 16 * h + 16]

    def put_big(out, base, counter, r, c, tile, turned):
        dest = owner(r, c) // 2
        slot = bump(counter + dest) + base

        @pl.when(c >= 6)
        def _():
            out[dest, slot] = tile

        @pl.when(c < 6)
        def _():
            out[dest, slot] = turned

    def step(t, _):
        r, c = row_col(pos, 0, me, t)
        tile = tiles[0, t]
        turned = tile.astype(f32).T.astype(bf16)

        @pl.when(jnp.logical_and(c < 6, r < 12))
        def _():
            par = lax.rem(c, 2)
            put_slab(turned, par, bump(48 + par))

        @pl.when(r >= 6)
        def _():
            put_big(big0, 0, 0, r, c, tile, turned)

        @pl.when(c >= 6)
        def _():
            er, ec = lifted(pb, r), lifted(pb, c)

            @pl.when(er < 6)
            def _():
                par = lax.rem(ec, 2)
                put_slab(turned, par, 9 + bump(50 + par))

            @pl.when(er >= 6)
            def _():
                put_big(bigm, 0, 16, er, ec, tile, turned)

        r, c = row_col(pos, 1, me, t)
        tile1 = tiles[1, t]
        turned1 = tile1.astype(f32).T.astype(bf16)

        @pl.when(r < 6)
        def _():
            par = lax.rem(c, 2)
            put_slab(turned1, par, 18 + bump(52 + par))

        @pl.when(r >= 6)
        def _():
            put_big(bigm, 6, 32, r, c, tile1, turned1)

        return 0

    lax.fori_loop(0, T, step, 0)


def pack(pos, pb, tiles):
    return pl.pallas_call(
        pack_kernel,
        out_shape=[
            jax.ShapeDtypeStruct((NF, 27, 16, TB), bf16),
            jax.ShapeDtypeStruct((NF, 6, TB, TB), bf16),
            jax.ShapeDtypeStruct((NF, 12, TB, TB), bf16),
        ],
        in_specs=[SM, SM, VM],
        out_specs=[VM, VM, VM],
        scratch_shapes=[pltpu.SMEM((64,), jnp.int32)],
        compiler_params=params(),
        name="pack",
    )(pos, pb, tiles)


def slab_kernel(pos, pb, x, diag, out):
    me = lax.axis_index("front")
    mine = me // 8
    out[...] = jnp.zeros_like(out)
    for i in range(4):
        out[54, i : i + 1] = diag[i : i + 1]

    def source(s, _):
        def step(t, counts):
            na, ne, nl = counts
            r, c = row_col(pos, 0, s, t)
            hit_a = jnp.logical_and(jnp.logical_and(c < 6, r < 12), lax.rem(c, 2) == mine)

            @pl.when(hit_a)
            def _():
                at = (c // 2) * 18 + r
                out[at] = out[at] + SCALE * x[s, na].astype(f32)

            er, ec = lifted(pb, r), lifted(pb, c)
            hit_e = jnp.logical_and(jnp.logical_and(c >= 6, er < 6), lax.rem(ec, 2) == mine)

            @pl.when(hit_e)
            def _():
                at = (ec // 2) * 18 + 12 + er
                out[at] = out[at] + SCALE * x[s, 9 + ne].astype(f32)

            r1, c1 = row_col(pos, 1, s, t)
            hit_l = jnp.logical_and(r1 < 6, lax.rem(c1, 2) == mine)

            @pl.when(hit_l)
            def _():
                at = (c1 // 2) * 18 + 12 + r1
                out[at] = out[at] + SCALE * x[s, 18 + nl].astype(f32)

            add = lambda n, hit: n + jnp.where(hit, 1, 0)
            return add(na, hit_a), add(ne, hit_e), add(nl, hit_l)

        zero = jnp.int32(0)
        lax.fori_loop(0, T, step, (zero, zero, zero))
        return 0

    lax.fori_loop(0, NF, source, 0)


def slab_sum(pos, pb, x, diag):
    return pl.pallas_call(
        slab_kernel,
        out_shape=f32s(56, 16, TB),
        in_specs=[SM, SM, VM, VM],
        out_specs=VM,
        compiler_params=params(),
        name="slab",
    )(pos, pb, x, diag)


def eye_mask():
    return lax.broadcasted_iota(jnp.int32, (TB, TB), 0) == lax.broadcasted_iota(
        jnp.int32, (TB, TB), 1
    )


def place(up, low, r, c, value):
    col = pl.multiple_of(lax.rem(owner(r, c), 2) * TB, TB)

    @pl.when(c >= 6)
    def _():
        row = pl.multiple_of((r - 6) * TB, TB)
        low[pl.ds(row, TB), pl.ds(col, TB)] = low[pl.ds(row, TB), pl.ds(col, TB)] + value

        @pl.when(r == c)
        def _():
            low[pl.ds(row, TB), pl.ds(col, TB)] = low[pl.ds(row, TB), pl.ds(col, TB)] + value.T

    @pl.when(c < 6)
    def _():
        row = pl.multiple_of(c * TB, TB)
        up[pl.ds(row, TB), pl.ds(col, TB)] = up[pl.ds(row, TB), pl.ds(col, TB)] + value


def add_diag(low, me, row0, row1):
    @pl.when(me >= 3)
    def _():
        for half, row in enumerate((row0, row1)):
            at = pl.multiple_of((me - 3) * B + half * TB, TB)
            cols = slice(half * TB, half * TB + TB)
            low[pl.ds(at, TB), cols] = low[pl.ds(at, TB), cols] + jnp.where(
                eye_mask(), jnp.broadcast_to(row, (TB, TB)), 0.0
            )


def leaf_kernel(pos, x, diag, up, low):
    me = lax.axis_index("front")
    up[...] = jnp.zeros_like(up)
    low[...] = jnp.zeros_like(low)

    def source(s, _):
        def step(t, n):
            r, c = row_col(pos, 0, s, t)
            hit = jnp.logical_and(r >= 6, owner(r, c) // 2 == me)

            @pl.when(hit)
            def _():
                place(up, low, r, c, SCALE * x[s, n].astype(f32))

            return n + jnp.where(hit, 1, 0)

        lax.fori_loop(0, T, step, jnp.int32(0))
        return 0

    lax.fori_loop(0, NF, source, 0)
    add_diag(low, me, diag[0:1], diag[1:2])


def leaf_assemble(pos, x, diag):
    return pl.pallas_call(
        leaf_kernel,
        out_shape=[f32s(PIV, B), f32s(F - PIV, B)],
        in_specs=[SM, VM, VM],
        out_specs=[VM, VM],
        compiler_params=params(),
        name="leafasm",
    )(pos, x, diag)


def parent_kernel(pos, pb, x, slab, diag, up, low):
    me = lax.axis_index("front")
    up[...] = jnp.zeros_like(up)
    low[...] = jnp.zeros_like(low)

    def source(s, _):
        def step(t, counts):
            ne, nl = counts
            r, c = row_col(pos, 0, s, t)
            er, ec = lifted(pb, r), lifted(pb, c)
            hit_e = jnp.logical_and(
                jnp.logical_and(c >= 6, er >= 6), owner(er, ec) // 2 == me
            )

            @pl.when(hit_e)
            def _():
                place(up, low, er, ec, SCALE * x[s, ne].astype(f32))

            r1, c1 = row_col(pos, 1, s, t)
            hit_l = jnp.logical_and(r1 >= 6, owner(r1, c1) // 2 == me)

            @pl.when(hit_l)
            def _():
                place(up, low, r1, c1, SCALE * x[s, 6 + nl].astype(f32))

            return ne + jnp.where(hit_e, 1, 0), nl + jnp.where(hit_l, 1, 0)

        zero = jnp.int32(0)
        lax.fori_loop(0, T, step, (zero, zero))
        return 0

    lax.fori_loop(0, NF, source, 0)
    add_diag(low, me, diag[2:3], diag[3:4])

    def extended(u, _):
        @pl.when(pb[u] == me)
        def _():
            rows = slab[u + 3, 54]
            add_diag(low, me, rows[0:1], rows[1:2])

        return 0

    lax.fori_loop(0, UB, extended, 0)


def parent_assemble(pos, pb, x, slab, diag):
    return pl.pallas_call(
        parent_kernel,
        out_shape=[f32s(PIV, B), f32s(F - PIV, B)],
        in_specs=[SM, SM, VM, VM, VM],
        out_specs=[VM, VM],
        compiler_params=params(),
        name="parentasm",
    )(pos, pb, x, slab, diag)


def lanes(x, j):
    return jnp.broadcast_to(x[:, j : j + 1], (8, TB))


def rows8(x, i):
    return jnp.broadcast_to(x[i : i + 1, :], (8, TB))


def factor_block(block):
    w = WIDTH
    s_rows = list(block)
    sub = lax.broadcasted_iota(jnp.int32, (8, TB), 0)
    lane = lax.broadcasted_iota(jnp.int32, (8, TB), 1)
    inv_rows = [(lane == sub + 8 * v).astype(f32) for v in range(16)]
    for k0 in range(0, TB, w):
        v0, s = k0 // 8, k0 % 8
        m = {(v, j): lanes(s_rows[v], k0 + j) for v in range(v0, 16) for j in range(w)}
        p = {(i, j): rows8(m[v0, j], s + i) for j in range(w) for i in range(j, w)}
        r_rows = [rows8(s_rows[v0], s + i) for i in range(w)]
        q_rows = [rows8(inv_rows[v0], s + i) for i in range(w)]
        low, scale = {}, []
        for j in range(w):
            d = p[j, j]
            for t in range(j):
                d = d - low[j, t] * low[j, t]
            rs = lax.rsqrt(d)
            scale.append(rs)
            for i in range(j + 1, w):
                x = p[i, j]
                for t in range(j):
                    x = x - low[i, t] * low[j, t]
                low[i, j] = x * rs
        us, ws = [], []
        for i in range(w):
            x, q = r_rows[i], q_rows[i]
            for t in range(i):
                x = x - low[i, t] * us[t]
                q = q - low[i, t] * ws[t]
            us.append(x * scale[i])
            ws.append(q * scale[i])
        for v in range(v0, 16):
            cs = []
            for i in range(w):
                x = m[v, i]
                for t in range(i):
                    x = x - low[i, t] * cs[t]
                cs.append(x * scale[i])
            if v == v0:
                cs = [jnp.where(sub >= s + w, x, 0.0) for x in cs]
            a, b = s_rows[v], inv_rows[v]
            for i in range(w):
                a = a - cs[i] * us[i]
                b = b - cs[i] * ws[i]
            if v == v0:
                for i in range(w):
                    a = jnp.where(sub == s + i, us[i], a)
                    b = jnp.where(sub == s + i, ws[i], b)
            s_rows[v], inv_rows[v] = a, b
    s_rows = [jnp.where(lane >= sub + 8 * v, s_rows[v], 0.0) for v in range(16)]
    return s_rows, inv_rows


def factor(a, u, li, n):
    for k in range(6):
        o = k * TB
        r = o + TB
        us, inv = factor_block([a[o + 8 * v : o + 8 * v + 8, o:r] for v in range(16)])
        for v in range(16):
            u[o + 8 * v : o + 8 * v + 8, o:r] = us[v]
            li[o + 8 * v : o + 8 * v + 8, :] = inv[v]
        if r < n:
            u[o:r, r:n] = dot(li[o:r, :], a[o:r, r:n], 1, 0)
            for q in range(r, PIV, TB):
                a[q : q + TB, q:n] = a[q : q + TB, q:n] - dot(
                    u[o:r, q : q + TB], u[o:r, q:n], 0, 0
                )


def first_kernel(pb, slab, own, u11, xt, p11, a, u, li):
    n = 2 * PIV + B

    def unpack(d, _):
        for cb in range(3):
            row = pl.multiple_of((2 * cb + d // 8) * TB + 16 * lax.rem(d, 8), 16)
            for k in range(12):
                a[pl.ds(row, 16), k * TB : k * TB + TB] = slab[d, cb * 18 + k]
            for k in range(6):
                p11[pl.ds(row, 16), k * TB : k * TB + TB] = slab[d, cb * 18 + 12 + k]
        return 0

    lax.fori_loop(0, NF, unpack, 0)
    eye = eye_mask()
    for b in range(6):
        cut = slice(b * TB, b * TB + TB)
        for ref, at in ((a, 0), (p11, 2)):
            block = ref[cut, cut]
            row = slab[b // 2, 54][at + b % 2 : at + b % 2 + 1]
            ref[cut, cut] = block + block.T + jnp.where(eye, jnp.broadcast_to(row, (TB, TB)), 0.0)
    a[:, 2 * PIV : n] = own[...]
    factor(a, u, li, n)
    u11[...] = u[:, :PIV]
    for i in range(6):
        for j in range(2):
            xt[j * TB : j * TB + TB, i * TB : i * TB + TB] = u[
                i * TB : i * TB + TB, 2 * PIV + j * TB : 2 * PIV + j * TB + TB
            ].T
    for v in range(3):

        @pl.when(pb[v] < 3)
        def _():
            to_col = pl.multiple_of(pb[v] * B, B)
            for half in range(2):
                at = pl.multiple_of(pb[v] * B + half * TB, TB)
                row = slab[v + 3, 54][half : half + 1]
                p11[pl.ds(at, TB), pl.ds(at, TB)] = p11[pl.ds(at, TB), pl.ds(at, TB)] + jnp.where(
                    eye, jnp.broadcast_to(row, (TB, TB)), 0.0
                )
            for w in range(v + 1):
                to_row = pl.multiple_of(pb[w] * B, B)
                gram = dot(
                    u[:, PIV + w * B : PIV + w * B + B], u[:, PIV + v * B : PIV + v * B + B], 0, 0
                )
                p11[pl.ds(to_row, B), pl.ds(to_col, B)] = (
                    p11[pl.ds(to_row, B), pl.ds(to_col, B)] - gram
                )


def first_factor(pb, slab, own):
    n = 2 * PIV + B
    return pl.pallas_call(
        first_kernel,
        out_shape=[f32s(PIV, PIV), f32s(B, PIV), f32s(PIV, PIV)],
        in_specs=[SM, VM, VM],
        out_specs=[VM, VM, VM],
        scratch_shapes=[
            pltpu.VMEM((PIV, n), f32),
            pltpu.VMEM((PIV, n), f32),
            pltpu.VMEM((PIV, TB), f32),
        ],
        compiler_params=params(),
        cost_estimate=pl.CostEstimate(
            flops=30_000_000_000, bytes_accessed=100_000_000, transcendentals=0
        ),
        name="first",
    )(pb, slab, own)


def second_kernel(own, other, u, li, a):
    a[...] = own[...] + other[...]
    factor(a, u, li, PIV)


def second_factor(own, other):
    return pl.pallas_call(
        second_kernel,
        out_shape=[f32s(PIV, PIV), f32s(PIV, TB)],
        in_specs=[VM, VM],
        out_specs=[VM, VM],
        scratch_shapes=[pltpu.VMEM((PIV, PIV), f32)],
        compiler_params=params(),
        cost_estimate=pl.CostEstimate(
            flops=20_000_000_000, bytes_accessed=100_000_000, transcendentals=0
        ),
        name="second",
    )(own, other)


def solve_kernel(u, li, own, other, xt, a):
    a[...] = own[...] + other[...]
    for k in range(6):
        o, r = k * TB, k * TB + TB
        x = dot(li[o:r, :], a[o:r, :], 1, 0)
        for j in range(2):
            xt[j * TB : j * TB + TB, o:r] = x[:, j * TB : j * TB + TB].T
        if r < PIV:
            a[r:, :] = a[r:, :] - dot(u[o:r, r:], x, 0, 0)


def solve(u, li, own, other):
    return pl.pallas_call(
        solve_kernel,
        out_shape=f32s(B, PIV),
        in_specs=[VM] * 4,
        out_specs=VM,
        scratch_shapes=[pltpu.VMEM((PIV, B), f32)],
        compiler_params=params(),
        name="solve",
    )(u, li, own, other)


def write_front(me, xall, u11, low, out):
    sub = lax.broadcasted_iota(jnp.int32, (B, B), 0)
    lane = lax.broadcasted_iota(jnp.int32, (B, B), 1)

    @pl.when(me >= 3)
    def _():
        def clear(k, _):
            out[pl.ds(pl.multiple_of(k * B, B), B), :] = jnp.zeros((B, B), f32)
            return 0

        lax.fori_loop(0, me, clear, 0)

        def update(k, _):
            at = pl.ds(pl.multiple_of((k - 3) * B, B), B)
            value = low(at) - dot(xall[k], xall[me], 1, 1)
            value = jnp.where(jnp.logical_or(k > me, sub >= lane), value, 0.0)
            out[pl.ds(pl.multiple_of(k * B, B), B), :] = value
            return 0

        lax.fori_loop(me, NF, update, 0)

    @pl.when(me < 3)
    def _():
        cols = pl.ds(pl.multiple_of(me * B, B), B)

        def copy(k, _):
            out[pl.ds(pl.multiple_of(k * B, B), B), :] = xall[k, :, cols]
            return 0

        lax.fori_loop(3, NF, copy, 0)
        for ib in range(6):
            for half in range(2):
                jb = 2 * me + half
                src = u11[pl.ds(pl.multiple_of(jb * TB, TB), TB), ib * TB : ib * TB + TB].T
                out[ib * TB : ib * TB + TB, half * TB : half * TB + TB] = jnp.where(
                    ib >= jb, src, 0.0
                )


def leaf_out_kernel(pb, xall, u11, alow, cup, clow, out, vup, vlow):
    me = lax.axis_index("front")
    vup[...] = cup[...]
    vlow[...] = clow[...]
    write_front(me, xall, u11, lambda at: alow[at, :], out)

    def column(v, _):
        @pl.when(jnp.logical_and(pb[v] == me, me >= 3))
        def _():
            def row(w, _):
                q = pb[w]

                @pl.when(q < 3)
                def _():
                    at = pl.ds(pl.multiple_of(q * B, B), B)
                    vup[at, :] = vup[at, :] - dot(xall[w + 3], xall[v + 3], 1, 1)

                @pl.when(q >= me)
                def _():
                    at = pl.ds(pl.multiple_of((q - 3) * B, B), B)
                    vlow[at, :] = vlow[at, :] - dot(xall[w + 3], xall[v + 3], 1, 1)

                return 0

            lax.fori_loop(0, UB, row, 0)

        return 0

    lax.fori_loop(0, UB, column, 0)


def leaf_output(pb, xall, u11, alow, cup, clow):
    return pl.pallas_call(
        leaf_out_kernel,
        out_shape=[f32s(F, B), f32s(PIV, B), f32s(F - PIV, B)],
        in_specs=[SM] + [VM] * 5,
        out_specs=[VM] * 3,
        compiler_params=params(),
        name="leafout",
    )(pb, xall, u11, alow, cup, clow)


def merged_out_kernel(xown, xother, u11, low0, low1, out, xall):
    me = lax.axis_index("front")
    core = lax.rem(lax.axis_index("leaf"), 2)
    mine = pl.ds(pl.multiple_of(core * TB, TB), TB)
    theirs = pl.ds(pl.multiple_of(TB - core * TB, TB), TB)

    def join(k, _):
        xall[k, mine, :] = xown[k]
        xall[k, theirs, :] = xother[k]
        return 0

    lax.fori_loop(3, NF, join, 0)
    write_front(me, xall, u11, lambda at: low0[at, :] + low1[at, :], out)


def merged_output(xown, xother, u11, low0, low1):
    return pl.pallas_call(
        merged_out_kernel,
        out_shape=f32s(F, B),
        in_specs=[VM] * 5,
        out_specs=VM,
        scratch_shapes=[pltpu.VMEM((NF, B, PIV), f32)],
        compiler_params=params(),
        name="mergedout",
    )(xown, xother, u11, low0, low1)


def gather_kernel(x, out, ss, rs, ls):
    me = lax.axis_index("front")
    y, z = me // 4, lax.rem(me, 4)

    def at(yy, zz):
        return lax.rem(yy + 8, 4) * 4 + lax.rem(zz + 8, 4)

    zr, zl, yr, yl = at(y, z + 1), at(y, z - 1), at(y + 1, z), at(y - 1, z)
    gate = pltpu.get_barrier_semaphore()
    for peer in (zr, zl, yr, yl):
        pl.semaphore_signal(gate, inc=1, device_id={"front": peer}, device_id_type=MESH)
    pl.semaphore_wait(gate, 4)
    half = x.shape[0] // 2
    part = half // 2
    own = pltpu.make_async_copy(x, out.at[me], ls)
    own.start()
    copies = []

    def send(src, dst, peer):
        i = len(copies)
        copy = pltpu.make_async_remote_copy(
            src_ref=src,
            dst_ref=dst,
            send_sem=ss.at[i],
            recv_sem=rs.at[i],
            device_id={"front": peer},
            device_id_type=MESH,
        )
        copy.start()
        copies.append(copy)
        return copy

    a, b = pl.ds(0, half), pl.ds(half, half)
    a0, a1 = pl.ds(0, part), pl.ds(part, part)
    b0, b1 = pl.ds(half, part), pl.ds(half + part, part)

    def pass_on(block, rows, peer):
        return send(out.at[block, rows], out.at[block, rows], peer)

    a1r = send(x.at[a], out.at[me, a], zr)
    a1l = send(x.at[a], out.at[me, a], zl)
    b1r = send(x.at[b], out.at[me, b], yr)
    b1l = send(x.at[b], out.at[me, b], yl)
    a1r.wait_recv()
    a2r = pass_on(zl, a0, zr)
    a1l.wait_recv()
    a2l = pass_on(zr, a1, zl)
    b1r.wait_recv()
    b2r = pass_on(yl, b0, yr)
    b1l.wait_recv()
    b2l = pass_on(yr, b1, yl)
    own.wait()
    zo, yo = at(y, z + 2), at(y + 2, z)
    ar, al, br, bl = [], [], [], []

    def second(block_a, block_b):
        ar.append(pass_on(block_a, a, yr))
        al.append(pass_on(block_a, a, yl))
        br.append(pass_on(block_b, b, zr))
        bl.append(pass_on(block_b, b, zl))

    second(me, me)
    second(zl, yl)
    second(zr, yr)
    for copy in (a2r, a2l, b2r, b2l):
        copy.wait_recv()
    second(zo, yo)
    last = []
    for q, o in enumerate((0, -1, 1, 2)):
        ar[q].wait_recv()
        last.append(pass_on(at(y - 1, z + o), a0, yr))
        al[q].wait_recv()
        last.append(pass_on(at(y + 1, z + o), a1, yl))
        br[q].wait_recv()
        last.append(pass_on(at(y + o, z - 1), b0, zr))
        bl[q].wait_recv()
        last.append(pass_on(at(y + o, z + 1), b1, zl))
    for copy in last:
        copy.wait_recv()
    for copy in copies:
        copy.wait_send()


def gather(x, number):
    return pl.pallas_call(
        gather_kernel,
        out_shape=jax.ShapeDtypeStruct((NF,) + x.shape, x.dtype),
        in_specs=[VM],
        out_specs=VM,
        scratch_shapes=[
            pltpu.SemaphoreType.DMA((40,)),
            pltpu.SemaphoreType.DMA((40,)),
            pltpu.SemaphoreType.DMA,
        ],
        compiler_params=params(collective_id=number, has_side_effects=True),
        name="gather%d" % number,
    )(x)


def exchange(x):
    route = [(i, i ^ 1) for i in range(lax.axis_size("leaf"))]
    return jax.tree.map(lambda v: lax.ppermute(v, "leaf", route), x)


def body(tiles, tile_pos, diag, parent_blocks):
    pos = tile_pos.reshape(-1)
    pb = parent_blocks.reshape(-1)
    diag = diag.reshape(4, TB)
    slab, big0, bigm = pack(pos, pb, tiles.reshape(2, T, TB, TB))
    to_all = lambda x: lax.all_to_all(x, "front", 0, 0, tiled=True)
    slab = slab_sum(pos, pb, to_all(slab), diag)
    slab = gather(slab.reshape(56 * 16, TB), 1).reshape(NF, 56, 16, TB)
    aup, alow = leaf_assemble(pos, to_all(big0), diag)
    u11, xt, p11 = first_factor(pb, slab, aup)
    xall = lax.all_gather(xt, "front")
    cup, clow = parent_assemble(pos, pb, to_all(bigm), slab, diag)
    m_u11, m_li = second_factor(p11, exchange(p11))
    leaf, vup, vlow = leaf_output(pb, xall, u11, alow, cup, clow)
    sup, slow = exchange((vup, vlow))
    m_xt = solve(m_u11, m_li, vup, sup)
    core = lax.rem(lax.axis_index("leaf"), 2)
    m_half = gather(lax.dynamic_slice_in_dim(m_xt, core * TB, TB, 0), 2)
    merged = merged_output(m_half, exchange(m_half), m_u11, vlow, slow)
    return leaf[None], merged[None]


def solution(mesh):
    placed = (
        P(None, "leaf", "front", None, None, None),
        P(None, "leaf", None, None, None),
        P(None, "leaf", "front"),
        P("leaf", None),
    )
    return jax.shard_map(
        body,
        mesh=mesh,
        in_specs=placed,
        out_specs=(P("leaf", None, "front"), P("leaf", None, "front")),
        check_vma=False,
    )
```

time: 1460 us -> 547 us (0.37)
  waiting for transfers between devices: 1130 us -> 144 us
  Pallas kernels: 0 us -> 324 us
  starting transfers between devices: 101 us -> 15.9 us
  other arithmetic: 64 us -> 0 us
  local copies, waits for them, and re-layouts: 63.1 us -> 8.37 us
  matrix products: 49.1 us -> 0 us
  blocking collectives: 0 us -> 30.2 us
  loops' own time: 26 us -> 0 us
    psum x6 -> x0, waiting for transfers between devices: 1040 us -> none  [from_root(): return lax.psum(kept, axis)]
    pallas_call x0 -> x11, Pallas kernels: none -> 324 us  [the longest x2 97.5 us: gather(): pl.pallas_call(gather_kernel, out_shape=jax.ShapeDtypeStruct((NF,) + x.sh...]
    all_to_all x3 -> x2, starting transfers between devices: 97.1 us -> 12.8 us  [body(): to_all = lambda x: lax.all_to_all(x, 'front', 0, 0, tiled=True)]
    dot_general x12 -> x0, matrix products: 49.1 us -> none  [the longest x6 35.2 us: factor_panels(): jnp.dot(panel_full[below_row:], rows_mine.T, precision=lax.Precision.HIGH...]
    select_n x13 -> x0, other arithmetic: 47.4 us -> none  [the longest x6 32.1 us: factor_panels(): jnp.where(front_index == owner_rank, matrix.at[:, offset:offset + B].set(...]
    all_gather x0 -> x1, waiting for transfers between devices: none -> 40.6 us  [body(): xall = lax.all_gather(xt, 'front')]
    all_to_all x0 -> x1, blocking collectives: none -> 30.2 us  [body(): to_all = lambda x: lax.all_to_all(x, 'front', 0, 0, tiled=True)]
    another operation x6 -> x0, loops' own time: 26 us -> none  [share_factored(): lax.cond(front_index == owner_rank, factor_panel, zeros_like_panel, column)]
  transfers between devices with their start and end apart: 10 -> 7, of which waited for: 9 -> 3; matrix products, arithmetic and copies ran while one was open for 3% -> 0% of each run, Pallas kernels for 0% -> 34%
where the time goes in v1:
time: 547 us; the launch traced here: 536 us
  Pallas kernels  324 us (59%)
  waiting for transfers between devices  144 us (26%)
  blocking collectives  30.2 us (6%)
  starting transfers between devices  15.9 us (3%)
  between operations  14.5 us (3%)
  local copies, waits for them, and re-layouts  8.37 us (2%)
    pallas_call x2, Pallas kernels, gather(): pl.pallas_call(gather_kernel, out_shape=jax.ShapeDtypeStruct((NF,) + x.sh...  97.5 us
    all_to_all x2, waiting for transfers between devices, body(): to_all = lambda x: lax.all_to_all(x, 'front', 0, 0, tiled=True)  88.3 us
    pallas_call x1, Pallas kernels, first_factor(): pl.pallas_call(first_kernel, out_shape=[f32s(PIV, PIV), f32s(B, PIV), f32...  46.2 us
    all_gather x1, waiting for transfers between devices, body(): xall = lax.all_gather(xt, 'front')  40.6 us
    pallas_call x1, Pallas kernels, second_factor(): pl.pallas_call(second_kernel, out_shape=[f32s(PIV, PIV), f32s(PIV, TB)],...  34.5 us
    pallas_call x1, Pallas kernels, leaf_output(): pl.pallas_call(leaf_out_kernel, out_shape=[f32s(F, B), f32s(PIV, B), f32s...  33.1 us
    pallas_call x1, Pallas kernels, parent_assemble(): pl.pallas_call(parent_kernel, out_shape=[f32s(PIV, B), f32s(F - PIV, B)],...  32.6 us
    all_to_all x1, blocking collectives, body(): to_all = lambda x: lax.all_to_all(x, 'front', 0, 0, tiled=True)  30.2 us
  transfers between devices with their start and end apart: 7, of which 3 were waited for; matrix products, arithmetic and copies ran while one was open for 0% of the time, Pallas kernels for 34%

profile of v1, /device:TPU:9, one launch (start us, length us, event | category | flops | bytes accessed | tf_op | source)
XLA Modules:
  0.0 536.3 jit_solution(17551437142685397999)
XLA Ops:
  7.2 1.4 reshape.23.pos
  8.6 11.5 %pack.1 = (bf16[16,27,16,128]{3,2,1,0:T(8,128)(2,1)}, bf16[16,6,128,128]{3,2,1,0:T(8,128)(2,1)}, bf16[16,12,128,128]{3,2,1,0:T(8,128)(2,1)}) custom-call(s32[1536]{0:T(1024)} %reshape.23.pos, s32[13]{0:T(128)} %bitcast.17, bf16[2,24,128,128]{3,2,1,0:T(8,128)(2,1)} %bitcast.13), custom_call_target="tpu_custom_call" | custom-call | tf_op jit(solution)/shard_map/pack/pallas_call | solution.py:131
  20.1 30.2 %all_to_all.15.x = bf16[16,27,16,128]{3,2,1,0:T(8,128)(2,1)} all-to-all(bf16[16,27,16,128]{3,2,1,0:T(8,128)(2,1)} %get-tuple-element.17), channel_id=1, replica_groups=mesh['leaf'=8,'front'=16] {'front'}, dimensions={0} | all-to-all | bytes 3538944 | tf_op jit(solution)/shard_map/all_to_all | solution.py:733
  50.3 5.0 all-to-all-start.1
  55.4 0.0 all-gather.3.cloned.1.call-start
  55.4 24.3 %slab.1 = f32[56,16,128]{2,1,0:T(8,128)} custom-call(s32[1536]{0:T(1024)} %reshape.23.pos, s32[13]{0:T(128)} %bitcast.18, bf16[16,27,16,128]{3,2,1,0:T(8,128)(2,1)} %all_to_all.15.x, f32[4,128]{1,0:T(4,128)} %bitcast.14), custom_call_target="tpu_custom_call" | custom-call | tf_op jit(solution)/shard_map/slab/pallas_call | solution.py:191
  79.7 57.4 %gather1.1 = f32[16,896,128]{2,1,0:T(8,128)} custom-call(f32[896,128]{1,0:T(8,128)} %bitcast.12), custom_call_target="tpu_custom_call" | custom-call | tf_op jit(solution)/shard_map/gather1/pallas_call | solution.py:708
  137.1 0.0 copy-start
  137.1 1.7 copy-done
  138.7 15.2 %leafasm.1 = (f32[768,256]{1,0:T(8,128)}, f32[3328,256]{1,0:T(8,128)}) custom-call(s32[1536]{0:T(1024)} %reshape.23.pos, bf16[16,6,128,128]{3,2,1,0:T(8,128)(2,1)} %copy-done, f32[4,128]{1,0:T(4,128)} %bitcast.15), custom_call_target="tpu_custom_call" | custom-call | tf_op jit(solution)/shard_map/leafasm/pallas_call | solution.py:260
  154.0 46.2 %first.1 = (f32[768,768]{1,0:T(8,128)}, f32[256,768]{1,0:T(8,128)}, f32[768,768]{1,0:T(8,128)}) custom-call(s32[13]{0:T(128)} %bitcast.19, f32[16,56,16,128]{3,2,1,0:T(8,128)} %bitcast.8, f32[768,256]{1,0:T(8,128)} %get-tuple-element.19.own), custom_call_target="tpu_custom_call" | custom-call | flops 30000001024 | bytes 100000000 | tf_op jit(solution)/shard_map/first/pallas_call | solution.py:455
  200.2 0.0 all-gather.3.cloned.1.call-update
  200.2 7.7 %all-to-all-start.2 = ((bf16[16,12,128,128]{3,2,1,0:T(8,128)(2,1)}), bf16[16,12,128,128]{3,2,1,0:T(8,128)(2,1)}, u32[]{:S(2)}, u32[]{:S(2)}) async-start(bf16[16,12,128,128]{3,2,1,0:T(8,128)(2,1)} %get-tuple-element.23), calls=%async_computation.2 | async-start | bytes 12582912 | tf_op jit(solution)/shard_map/all_to_all | solution.py:733
  208.0 1.0 collective-permute-start
  209.0 88.3 %all-to-all-done.2.x = bf16[16,12,128,128]{3,2,1,0:T(8,128)(2,1)} async-done(((bf16[16,12,128,128]{3,2,1,0:T(8,128)(2,1)}), bf16[16,12,128,128]{3,2,1,0:T(8,128)(2,1)}, u32[]{:S(2)}, u32[]{:S(2)}) %all-to-all-start.2) | async-done | bytes 6291488 | tf_op jit(solution)/shard_map/all_to_all | solution.py:733
  297.3 32.6 %parentasm.1 = (f32[768,256]{1,0:T(8,128)}, f32[3328,256]{1,0:T(8,128)}) custom-call(s32[1536]{0:T(1024)} %reshape.23.pos, s32[13]{0:T(128)} %bitcast.20, bf16[16,12,128,128]{3,2,1,0:T(8,128)(2,1)} %all-to-all-done.2.x, f32[16,56,16,128]{3,2,1,0:T(8,128)} %bitcast.9, f32[4,128]{1,0:T(4,128)} %bitcast.16), custom_call_target="tpu_custom_call" | custom-call | tf_op jit(solution)/shard_map/parentasm/pallas_call | solution.py:316
  329.9 40.6 %all-gather.3.cloned.1.call-done = f32[4096,768]{1,0:T(8,128)} async-done(((f32[256,768]{1,0:T(8,128)}), f32[4096,768]{1,0:T(8,128)}) %all-gather.3.cloned.1.call-update) | async-done | bytes 12582928 | tf_op jit(solution)/shard_map/all_gather | solution.py:738
  370.5 33.1 %leafout.1 = (f32[4096,256]{1,0:T(8,128)}, f32[768,256]{1,0:T(8,128)}, f32[3328,256]{1,0:T(8,128)}) custom-call(s32[13]{0:T(128)} %bitcast.21, f32[16,256,768]{2,1,0:T(8,128)} %bitcast.10, f32[768,768]{1,0:T(8,128)} %get-tuple-element.21.u11, f32[3328,256]{1,0:T(8,128)} %get-tuple-element.22.alow, f32[768,256]{1,0:T(8,128)} %get-tuple-element.24.cup, ...), custom_call_target="tpu_custom_call" | custom-call | tf_op jit(solution)/shard_map/leafout/pallas_call | solution.py:587
  403.6 0.2 collective-permute-start.1
  403.7 0.0 collective-permute-done.other
  403.7 34.5 %second.1 = (f32[768,768]{1,0:T(8,128)}, f32[768,128]{1,0:T(8,128)}) custom-call(f32[768,768]{1,0:T(8,128)} %get-tuple-element.27.own, f32[768,768]{1,0:T(8,128)} %collective-permute-done.other), custom_call_target="tpu_custom_call" | custom-call | flops 20000000000 | bytes 100000000 | tf_op jit(solution)/shard_map/second/pallas_call | solution.py:479
  438.3 0.0 collective-permute-done.1.other
  438.3 0.9 copy-done.2
  439.1 8.3 %solve.1 = f32[256,768]{1,0:T(8,128)} custom-call(f32[768,768]{1,0:T(8,128)} %get-tuple-element.28.u.u11, f32[768,128]{1,0:T(8,128)} %get-tuple-element.29.li, f32[768,256]{1,0:T(8,128)} %get-tuple-element.30.own, f32[768,256]{1,0:T(8,128)} %copy-done.2), custom_call_target="tpu_custom_call" | custom-call | tf_op jit(solution)/shard_map/solve/pallas_call | solution.py:505
  447.4 1.8 constant_dynamic-slice_fusion.x
  449.2 40.1 %gather2.1.xown = f32[16,128,768]{2,1,0:T(8,128)} custom-call(f32[128,768]{1,0:T(8,128)} %constant_dynamic-slice_fusion.x), custom_call_target="tpu_custom_call" | custom-call | tf_op jit(solution)/shard_map/gather2/pallas_call | solution.py:708
  489.3 1.9 collective-permute-start.2
  491.2 0.1 collective-permute-start.3
  491.3 14.8 %collective-permute-done.3.low1 = f32[3328,256]{1,0:T(8,128)} collective-permute-done((f32[3328,256]{1,0:T(8,128)}, f32[3328,256]{1,0:T(8,128)}, u32[]{:S(2)}, u32[]{:S(2)}) %collective-permute-start.3) | collective-permute-done | bytes 3407904 | tf_op jit(solution)/shard_map/ppermute | solution.py:725
  506.1 0.0 collective-permute-done.2.xother
  506.1 2.6 copy-done.1
  508.7 20.4 %mergedout.1 = f32[4096,256]{1,0:T(8,128)} custom-call(f32[16,128,768]{2,1,0:T(8,128)} %gather2.1.xown, f32[16,128,768]{2,1,0:T(8,128)} %copy-done.1, f32[768,768]{1,0:T(8,128)} %get-tuple-element.28.u.u11, f32[3328,256]{1,0:T(8,128)} %get-tuple-element.31.low0, f32[3328,256]{1,0:T(8,128)} %collective-permute-done.3.low1), custom_call_target="tpu_custom_call" | custom-call | tf_op jit(solution)/shard_map/mergedout/pallas_call | solution.py:613
  (5 shorter events, 0.0 us)
Async XLA Ops:
  50.3 86.7 %all-to-all-start.1 = ((bf16[16,6,128,128]{3,2,1,0:T(8,128)(2,1)}), bf16[16,6,128,128]{3,2,1,0:T(8,128)(2,1)S(1)}, u32[]{:S(2)}, u32[]{:S(2)}) async-start(bf16[16,6,128,128]{3,2,1,0:T(8,128)(2,1)} %get-tuple-element.18), calls=%async_computation.1 | async-start | bytes 6291456 | tf_op jit(solution)/shard_map/all_to_all | solution.py:733
  55.4 315.1 %all-gather.3.cloned.1.call-start = ((), (), s32[]{:S(2)}) async-start(), calls=%async_computation.3 | async-start | bytes 13369344 | tf_op jit(solution)/shard_map/all_gather | solution.py:738
  137.1 1.7 copy-start
  200.2 7.8 %copy-start.3 = (f32[768,768]{1,0:T(8,128)S(1)}, f32[768,768]{1,0:T(8,128)}, u32[]{:S(2)}) copy-start(f32[768,768]{1,0:T(8,128)} %get-tuple-element.27.own) | copy-start | bytes 7077892
  200.2 97.0 %all-to-all-start.2 = ((bf16[16,12,128,128]{3,2,1,0:T(8,128)(2,1)}), bf16[16,12,128,128]{3,2,1,0:T(8,128)(2,1)}, u32[]{:S(2)}, u32[]{:S(2)}) async-start(bf16[16,12,128,128]{3,2,1,0:T(8,128)(2,1)} %get-tuple-element.23), calls=%async_computation.2 | async-start | bytes 12582912 | tf_op jit(solution)/shard_map/all_to_all | solution.py:733
  208.0 195.8 %collective-permute-start = (f32[768,768]{1,0:T(8,128)S(1)}, f32[768,768]{1,0:T(8,128)}, u32[]{:S(2)}, u32[]{:S(2)}) collective-permute-start(f32[768,768]{1,0:T(8,128)S(1)} %copy-done.3), channel_id=1, source_target_pairs={{0,16},{16,0},{32,48},{48,32},{64,80},{80,64},{96,112},{112,96},{1... | collective-permute-start | bytes 7077896 | tf_op jit(solution)/shard_map/ppermute | solution.py:725
  403.6 34.7 %collective-permute-start.1 = (f32[768,256]{1,0:T(8,128)}, f32[768,256]{1,0:T(8,128)S(1)}, u32[]{:S(2)}, u32[]{:S(2)}) collective-permute-start(f32[768,256]{1,0:T(8,128)} %get-tuple-element.30.own), channel_id=1, source_target_pairs={{0,16},{16,0},{32,48},{48,32},{64,80},{80,64},{96,112},{112,96},{1... | collective-permute-start | bytes 2359304 | tf_op jit(solution)/shard_map/ppermute | solution.py:725
  438.3 0.9 copy-start.2
  489.3 16.8 %collective-permute-start.2 = (f32[16,128,768]{2,1,0:T(8,128)}, f32[16,128,768]{2,1,0:T(8,128)S(1)}, u32[]{:S(2)}, u32[]{:S(2)}) collective-permute-start(f32[16,128,768]{2,1,0:T(8,128)} %gather2.1.xown), channel_id=1, source_target_pairs={{0,16},{16,0},{32,48},{48,32},{64,80},{80,64},{96,112},{112,96},{1... | collective-permute-start | bytes 18874376 | tf_op jit(solution)/shard_map/ppermute | solution.py:725
  491.2 14.9 %collective-permute-start.3 = (f32[3328,256]{1,0:T(8,128)}, f32[3328,256]{1,0:T(8,128)}, u32[]{:S(2)}, u32[]{:S(2)}) collective-permute-start(f32[3328,256]{1,0:T(8,128)} %get-tuple-element.31.low0), channel_id=1, source_target_pairs={{0,16},{16,0},{32,48},{48,32},{64,80},{80,64},{96,112},{112,96},{1... | collective-permute-start | bytes 10223624 | tf_op jit(solution)/shard_map/ppermute | solution.py:725
  506.1 2.6 copy-start.1
Sparse Core Ops, SparseCore 0:
  200.3 170.0 all-gather.2

commit v2 on v1

--- a/solution.py
+++ b/solution.py
@@ -21,6 +21,7 @@
 bf16 = jnp.bfloat16
 VM = pl.BlockSpec(memory_space=pltpu.VMEM)
 SM = pl.BlockSpec(memory_space=pltpu.SMEM)
+ANY = pl.BlockSpec(memory_space=pl.ANY)
 LIMIT = 56 << 20
 WIDTH = 8
 
@@ -143,59 +144,94 @@
     )(pos, pb, tiles)
 
 
-def slab_kernel(pos, pb, x, diag, out):
+def plan_kernel(pb, pos, out):
     me = lax.axis_index("front")
-    mine = me // 8
+    half = me // 8
+    r0, c0, r1, c1 = pos[0, 0], pos[0, 1], pos[1, 0], pos[1, 1]
+
+    def lift(x):
+        block = jnp.maximum(x - 6, 0) // 2
+        to = jnp.zeros_like(x)
+        for u in range(UB):
+            to = jnp.where(block == u, pb[u], to)
+        return 2 * to + lax.rem(x, 2)
+
+    er, ec = lift(r0), lift(c0)
+
+    def slab_code(c, r, start, slope):
+        cb = c // 2
+        return start + r + slope * cb - cb * cb
+
+    def own_code(r, c):
+        row = jnp.where(c >= 6, r, c)
+        return 4 * row + 2 * lax.rem(owner(r, c), 2) + jnp.where(r == c, 1, 0)
+
+    def own_hit(r, c):
+        return (r >= 6) & (owner(r, c) // 2 == me)
+
+    sets = (
+        ((c0 < 6) & (r0 < 12) & (lax.rem(c0, 2) == half), slab_code(c0, r0, 0, 11)),
+        ((c0 >= 6) & (er < 6) & (lax.rem(ec, 2) == half), slab_code(ec, er, 30, 5)),
+        ((r1 < 6) & (lax.rem(c1, 2) == half), slab_code(c1, r1, 30, 5)),
+        (own_hit(r0, c0), own_code(r0, c0)),
+        ((c0 >= 6) & own_hit(er, ec), own_code(er, ec)),
+        (own_hit(r1, c1), own_code(r1, c1)),
+    )
+    before = lax.broadcasted_iota(jnp.int32, (T, T), 0) < lax.broadcasted_iota(
+        jnp.int32, (T, T), 1
+    )
+    before = before.astype(f32)
+    lane = lax.broadcasted_iota(jnp.int32, (NF, TB), 1)
+    for i, (hit, code) in enumerate(sets):
+        one = jnp.where(hit, 1.0, 0.0)
+        rank = dot(one, before, 1, 0)
+        code = code.astype(f32)
+        table = jnp.where(lane == TB - 1, jnp.sum(one, axis=1, keepdims=True), 0.0)
+        for k in range(9):
+            pick = jnp.where(rank == k, one * code, 0.0)
+            table = jnp.where(lane == k, jnp.sum(pick, axis=1, keepdims=True), table)
+        out[NF * i : NF * i + NF, :] = (table + 0.5).astype(jnp.int32)
+
+
+def make_plan(pb, pos):
+    return pl.pallas_call(
+        plan_kernel,
+        out_shape=jax.ShapeDtypeStruct((6 * NF, TB), jnp.int32),
+        in_specs=[SM, VM],
+        out_specs=VM,
+        compiler_params=params(),
+        name="plan",
+    )(pb, pos)
+
+
+def slab_kernel(plan, x, diag, out):
     out[...] = jnp.zeros_like(out)
     for i in range(4):
-        out[54, i : i + 1] = diag[i : i + 1]
+        out[42, i : i + 1] = diag[i : i + 1]
 
     def source(s, _):
-        def step(t, counts):
-            na, ne, nl = counts
-            r, c = row_col(pos, 0, s, t)
-            hit_a = jnp.logical_and(jnp.logical_and(c < 6, r < 12), lax.rem(c, 2) == mine)
-
-            @pl.when(hit_a)
-            def _():
-                at = (c // 2) * 18 + r
-                out[at] = out[at] + SCALE * x[s, na].astype(f32)
-
-            er, ec = lifted(pb, r), lifted(pb, c)
-            hit_e = jnp.logical_and(jnp.logical_and(c >= 6, er < 6), lax.rem(ec, 2) == mine)
-
-            @pl.when(hit_e)
-            def _():
-                at = (ec // 2) * 18 + 12 + er
-                out[at] = out[at] + SCALE * x[s, 9 + ne].astype(f32)
-
-            r1, c1 = row_col(pos, 1, s, t)
-            hit_l = jnp.logical_and(r1 < 6, lax.rem(c1, 2) == mine)
-
-            @pl.when(hit_l)
-            def _():
-                at = (c1 // 2) * 18 + 12 + r1
-                out[at] = out[at] + SCALE * x[s, 18 + nl].astype(f32)
-
-            add = lambda n, hit: n + jnp.where(hit, 1, 0)
-            return add(na, hit_a), add(ne, hit_e), add(nl, hit_l)
-
-        zero = jnp.int32(0)
-        lax.fori_loop(0, T, step, (zero, zero, zero))
+        for i in range(3):
+
+            def add(k, _, i=i):
+                at = plan[i * NF + s, k]
+                out[at] = out[at] + SCALE * x[s, 9 * i + k].astype(f32)
+                return 0
+
+            lax.fori_loop(0, plan[i * NF + s, TB - 1], add, 0)
         return 0
 
     lax.fori_loop(0, NF, source, 0)
 
 
-def slab_sum(pos, pb, x, diag):
+def slab_sum(plan, x, diag):
     return pl.pallas_call(
         slab_kernel,
-        out_shape=f32s(56, 16, TB),
-        in_specs=[SM, SM, VM, VM],
+        out_shape=f32s(44, 16, TB),
+        in_specs=[SM, VM, VM],
         out_specs=VM,
         compiler_params=params(),
         name="slab",
-    )(pos, pb, x, diag)
+    )(plan, x, diag)
 
 
 def eye_mask():
@@ -204,22 +240,23 @@
     )
 
 
-def place(up, low, r, c, value):
-    col = pl.multiple_of(lax.rem(owner(r, c), 2) * TB, TB)
-
-    @pl.when(c >= 6)
+def place(up, low, code, value):
+    row = code // 4
+    col = pl.ds(pl.multiple_of(lax.rem(code // 2, 2) * TB, TB), TB)
+
+    @pl.when(row >= 6)
     def _():
-        row = pl.multiple_of((r - 6) * TB, TB)
-        low[pl.ds(row, TB), pl.ds(col, TB)] = low[pl.ds(row, TB), pl.ds(col, TB)] + value
-
-        @pl.when(r == c)
-        def _():
-            low[pl.ds(row, TB), pl.ds(col, TB)] = low[pl.ds(row, TB), pl.ds(col, TB)] + value.T
-
-    @pl.when(c < 6)
+        at = pl.ds(pl.multiple_of((row - 6) * TB, TB), TB)
+        low[at, col] = low[at, col] + value
+
+        @pl.when(lax.rem(code, 2) == 1)
+        def _():
+            low[at, col] = low[at, col] + value.T
+
+    @pl.when(row < 6)
     def _():
-        row = pl.multiple_of(c * TB, TB)
-        up[pl.ds(row, TB), pl.ds(col, TB)] = up[pl.ds(row, TB), pl.ds(col, TB)] + value
+        at = pl.ds(pl.multiple_of(row * TB, TB), TB)
+        up[at, col] = up[at, col] + value
 
 
 def add_diag(low, me, row0, row1):
@@ -233,78 +270,50 @@
             )
 
 
-def leaf_kernel(pos, x, diag, up, low):
-    me = lax.axis_index("front")
+def gather_tiles(plan, x, up, low, sets):
+    first = sets[0]
     up[...] = jnp.zeros_like(up)
     low[...] = jnp.zeros_like(low)
 
     def source(s, _):
-        def step(t, n):
-            r, c = row_col(pos, 0, s, t)
-            hit = jnp.logical_and(r >= 6, owner(r, c) // 2 == me)
-
-            @pl.when(hit)
-            def _():
-                place(up, low, r, c, SCALE * x[s, n].astype(f32))
-
-            return n + jnp.where(hit, 1, 0)
-
-        lax.fori_loop(0, T, step, jnp.int32(0))
+        for i in sets:
+
+            def add(k, _, i=i):
+                place(up, low, plan[i * NF + s, k], SCALE * x[s, 6 * (i - first) + k].astype(f32))
+                return 0
+
+            lax.fori_loop(0, plan[i * NF + s, TB - 1], add, 0)
         return 0
 
     lax.fori_loop(0, NF, source, 0)
+
+
+def leaf_kernel(plan, x, diag, after, up, low):
+    me = lax.axis_index("front")
+    gather_tiles(plan, x, up, low, (3,))
     add_diag(low, me, diag[0:1], diag[1:2])
 
 
-def leaf_assemble(pos, x, diag):
+def leaf_assemble(plan, x, diag, after):
     return pl.pallas_call(
         leaf_kernel,
         out_shape=[f32s(PIV, B), f32s(F - PIV, B)],
-        in_specs=[SM, VM, VM],
+        in_specs=[SM, VM, VM, ANY],
         out_specs=[VM, VM],
         compiler_params=params(),
         name="leafasm",
-    )(pos, x, diag)
-
-
-def parent_kernel(pos, pb, x, slab, diag, up, low):
+    )(plan, x, diag, after)
+
+
+def parent_kernel(plan, pb, x, extra, diag, after, up, low):
     me = lax.axis_index("front")
-    up[...] = jnp.zeros_like(up)
-    low[...] = jnp.zeros_like(low)
-
-    def source(s, _):
-        def step(t, counts):
-            ne, nl = counts
-            r, c = row_col(pos, 0, s, t)
-            er, ec = lifted(pb, r), lifted(pb, c)
-            hit_e = jnp.logical_and(
-                jnp.logical_and(c >= 6, er >= 6), owner(er, ec) // 2 == me
-            )
-
-            @pl.when(hit_e)
-            def _():
-                place(up, low, er, ec, SCALE * x[s, ne].astype(f32))
-
-            r1, c1 = row_col(pos, 1, s, t)
-            hit_l = jnp.logical_and(r1 >= 6, owner(r1, c1) // 2 == me)
-
-            @pl.when(hit_l)
-            def _():
-                place(up, low, r1, c1, SCALE * x[s, 6 + nl].astype(f32))
-
-            return ne + jnp.where(hit_e, 1, 0), nl + jnp.where(hit_l, 1, 0)
-
-        zero = jnp.int32(0)
-        lax.fori_loop(0, T, step, (zero, zero))
-        return 0
-
-    lax.fori_loop(0, NF, source, 0)
+    gather_tiles(plan, x, up, low, (4, 5))
     add_diag(low, me, diag[2:3], diag[3:4])
 
     def extended(u, _):
         @pl.when(pb[u] == me)
         def _():
-            rows = slab[u + 3, 54]
+            rows = extra[u + 3]
             add_diag(low, me, rows[0:1], rows[1:2])
 
         return 0
@@ -312,15 +321,15 @@
     lax.fori_loop(0, UB, extended, 0)
 
 
-def parent_assemble(pos, pb, x, slab, diag):
+def parent_assemble(plan, pb, x, extra, diag, after):
     return pl.pallas_call(
         parent_kernel,
         out_shape=[f32s(PIV, B), f32s(F - PIV, B)],
-        in_specs=[SM, SM, VM, VM, VM],
+        in_specs=[SM, SM, VM, VM, VM, ANY],
         out_specs=[VM, VM],
         compiler_params=params(),
         name="parentasm",
-    )(pos, pb, x, slab, diag)
+    )(plan, pb, x, extra, diag, after)
 
 
 def lanes(x, j):
@@ -401,16 +410,17 @@
                 )
 
 
-def first_kernel(pb, slab, own, u11, xt, p11, a, u, li):
-    n = 2 * PIV + B
+def first_kernel(pb, slab, after, u11, p11, li, a, u):
+    n = 2 * PIV
+    p11[...] = jnp.zeros_like(p11)
 
     def unpack(d, _):
         for cb in range(3):
             row = pl.multiple_of((2 * cb + d // 8) * TB + 16 * lax.rem(d, 8), 16)
-            for k in range(12):
-                a[pl.ds(row, 16), k * TB : k * TB + TB] = slab[d, cb * 18 + k]
-            for k in range(6):
-                p11[pl.ds(row, 16), k * TB : k * TB + TB] = slab[d, cb * 18 + 12 + k]
+            for k in range(2 * cb, 12):
+                a[pl.ds(row, 16), k * TB : k * TB + TB] = slab[d, 11 * cb - cb * cb + k]
+            for k in range(2 * cb, 6):
+                p11[pl.ds(row, 16), k * TB : k * TB + TB] = slab[d, 30 + 5 * cb - cb * cb + k]
         return 0
 
     lax.fori_loop(0, NF, unpack, 0)
@@ -419,16 +429,10 @@
         cut = slice(b * TB, b * TB + TB)
         for ref, at in ((a, 0), (p11, 2)):
             block = ref[cut, cut]
-            row = slab[b // 2, 54][at + b % 2 : at + b % 2 + 1]
+            row = slab[b // 2, 42][at + b % 2 : at + b % 2 + 1]
             ref[cut, cut] = block + block.T + jnp.where(eye, jnp.broadcast_to(row, (TB, TB)), 0.0)
-    a[:, 2 * PIV : n] = own[...]
     factor(a, u, li, n)
     u11[...] = u[:, :PIV]
-    for i in range(6):
-        for j in range(2):
-            xt[j * TB : j * TB + TB, i * TB : i * TB + TB] = u[
-                i * TB : i * TB + TB, 2 * PIV + j * TB : 2 * PIV + j * TB + TB
-            ].T
     for v in range(3):
 
         @pl.when(pb[v] < 3)
@@ -436,7 +440,7 @@
             to_col = pl.multiple_of(pb[v] * B, B)
             for half in range(2):
                 at = pl.multiple_of(pb[v] * B + half * TB, TB)
-                row = slab[v + 3, 54][half : half + 1]
+                row = slab[v + 3, 42][half : half + 1]
                 p11[pl.ds(at, TB), pl.ds(at, TB)] = p11[pl.ds(at, TB), pl.ds(at, TB)] + jnp.where(
                     eye, jnp.broadcast_to(row, (TB, TB)), 0.0
                 )
@@ -450,24 +454,17 @@
                 )
 
 
-def first_factor(pb, slab, own):
-    n = 2 * PIV + B
+def first_factor(pb, slab, after):
+    n = 2 * PIV
     return pl.pallas_call(
         first_kernel,
-        out_shape=[f32s(PIV, PIV), f32s(B, PIV), f32s(PIV, PIV)],
-        in_specs=[SM, VM, VM],
+        out_shape=[f32s(PIV, PIV), f32s(PIV, PIV), f32s(PIV, TB)],
+        in_specs=[SM, VM, ANY],
         out_specs=[VM, VM, VM],
-        scratch_shapes=[
-            pltpu.VMEM((PIV, n), f32),
-            pltpu.VMEM((PIV, n), f32),
-            pltpu.VMEM((PIV, TB), f32),
-        ],
-        compiler_params=params(),
-        cost_estimate=pl.CostEstimate(
-            flops=30_000_000_000, bytes_accessed=100_000_000, transcendentals=0
-        ),
+        scratch_shapes=[pltpu.VMEM((PIV, n), f32), pltpu.VMEM((PIV, n), f32)],
+        compiler_params=params(),
         name="first",
-    )(pb, slab, own)
+    )(pb, slab, after)
 
 
 def second_kernel(own, other, u, li, a):
@@ -483,15 +480,13 @@
         out_specs=[VM, VM],
         scratch_shapes=[pltpu.VMEM((PIV, PIV), f32)],
         compiler_params=params(),
-        cost_estimate=pl.CostEstimate(
-            flops=20_000_000_000, bytes_accessed=100_000_000, transcendentals=0
-        ),
         name="second",
     )(own, other)
 
 
-def solve_kernel(u, li, own, other, xt, a):
-    a[...] = own[...] + other[...]
+def solve_kernel(n, u, li, *refs):
+    terms, (xt, a) = refs[:n], refs[-2:]
+    a[...] = sum((t[...] for t in terms[1:]), terms[0][...])
     for k in range(6):
         o, r = k * TB, k * TB + TB
         x = dot(li[o:r, :], a[o:r, :], 1, 0)
@@ -501,16 +496,29 @@
             a[r:, :] = a[r:, :] - dot(u[o:r, r:], x, 0, 0)
 
 
-def solve(u, li, own, other):
-    return pl.pallas_call(
-        solve_kernel,
+def solve(u, li, terms, after=()):
+    return pl.pallas_call(
+        functools.partial(solve_kernel, len(terms)),
         out_shape=f32s(B, PIV),
-        in_specs=[VM] * 4,
+        in_specs=[VM] * (2 + len(terms)) + [ANY] * len(after),
         out_specs=VM,
         scratch_shapes=[pltpu.VMEM((PIV, B), f32)],
         compiler_params=params(),
-        name="solve",
-    )(u, li, own, other)
+        name="solve%d" % len(terms),
+    )(u, li, *terms, *after)
+
+
+def split(x):
+    high = x.astype(bf16)
+    return high, (x - high.astype(f32)).astype(bf16)
+
+
+def product(x, y):
+    (xh, xl), (yh, yl) = x, y
+    one = lambda p, q: lax.dot_general(
+        p, q, (((1,), (1,)), ((), ())), preferred_element_type=f32
+    )
+    return one(xh, yh) + (one(xh, yl) + one(xl, yh))
 
 
 def write_front(me, xall, u11, low, out):
@@ -525,9 +533,11 @@
 
         lax.fori_loop(0, me, clear, 0)
 
+        mine = split(xall[me])
+
         def update(k, _):
             at = pl.ds(pl.multiple_of((k - 3) * B, B), B)
-            value = low(at) - dot(xall[k], xall[me], 1, 1)
+            value = low(at) - product(split(xall[k]), mine)
             value = jnp.where(jnp.logical_or(k > me, sub >= lane), value, 0.0)
             out[pl.ds(pl.multiple_of(k * B, B), B), :] = value
             return 0
@@ -552,15 +562,16 @@
                 )
 
 
-def leaf_out_kernel(pb, xall, u11, alow, cup, clow, out, vup, vlow):
+def extend_kernel(pb, xall, cup, clow, vup, vlow):
     me = lax.axis_index("front")
     vup[...] = cup[...]
     vlow[...] = clow[...]
-    write_front(me, xall, u11, lambda at: alow[at, :], out)
 
     def column(v, _):
         @pl.when(jnp.logical_and(pb[v] == me, me >= 3))
         def _():
+            mine = split(xall[v + 3])
+
             def row(w, _):
                 q = pb[w]
 
@@ -572,7 +583,7 @@
                 @pl.when(q >= me)
                 def _():
                     at = pl.ds(pl.multiple_of((q - 3) * B, B), B)
-                    vlow[at, :] = vlow[at, :] - dot(xall[w + 3], xall[v + 3], 1, 1)
+                    vlow[at, :] = vlow[at, :] - product(split(xall[w + 3]), mine)
 
                 return 0
 
@@ -583,15 +594,33 @@
     lax.fori_loop(0, UB, column, 0)
 
 
-def leaf_output(pb, xall, u11, alow, cup, clow):
+def extend_add(pb, xall, cup, clow):
+    return pl.pallas_call(
+        extend_kernel,
+        out_shape=[f32s(PIV, B), f32s(F - PIV, B)],
+        in_specs=[SM] + [VM] * 3,
+        out_specs=[VM] * 2,
+        compiler_params=params(),
+        name="extend",
+    )(pb, xall, cup, clow)
+
+
+def leaf_out_kernel(xall, u11, alow, after, out):
+    write_front(lax.axis_index("front"), xall, u11, lambda at: alow[at, :], out)
+
+
+def leaf_output(xall, u11, alow, after):
     return pl.pallas_call(
         leaf_out_kernel,
-        out_shape=[f32s(F, B), f32s(PIV, B), f32s(F - PIV, B)],
-        in_specs=[SM] + [VM] * 5,
-        out_specs=[VM] * 3,
-        compiler_params=params(),
+        out_shape=f32s(F, B),
+        in_specs=[VM] * 3 + [ANY],
+        out_specs=VM,
+        compiler_params=params(),
+        cost_estimate=pl.CostEstimate(
+            flops=8_000_000_000, bytes_accessed=30_000_000, transcendentals=0
+        ),
         name="leafout",
-    )(pb, xall, u11, alow, cup, clow)
+    )(xall, u11, alow, after)
 
 
 def merged_out_kernel(xown, xother, u11, low0, low1, out, xall):
@@ -730,19 +759,26 @@
     pb = parent_blocks.reshape(-1)
     diag = diag.reshape(4, TB)
     slab, big0, bigm = pack(pos, pb, tiles.reshape(2, T, TB, TB))
+    plan = make_plan(pb, jnp.transpose(tile_pos[:, 0], (0, 2, 1, 3)))
     to_all = lambda x: lax.all_to_all(x, "front", 0, 0, tiled=True)
-    slab = slab_sum(pos, pb, to_all(slab), diag)
-    slab = gather(slab.reshape(56 * 16, TB), 1).reshape(NF, 56, 16, TB)
-    aup, alow = leaf_assemble(pos, to_all(big0), diag)
-    u11, xt, p11 = first_factor(pb, slab, aup)
+    slab = slab_sum(plan, to_all(slab), diag)
+    big0 = to_all(big0)
+    slab = gather(slab.reshape(44 * 16, TB), 1)
+    slab, bigm = lax.optimization_barrier((slab, bigm))
+    slab = slab.reshape(NF, 44, 16, TB)
+    bigm = to_all(bigm)
+    aup, alow = leaf_assemble(plan, big0, diag, slab)
+    u11, p11, li = first_factor(pb, slab, aup)
+    m_u11, m_li = second_factor(p11, exchange(p11))
+    xt = solve(u11, li, (aup,), (m_li, bigm))
     xall = lax.all_gather(xt, "front")
-    cup, clow = parent_assemble(pos, pb, to_all(bigm), slab, diag)
-    m_u11, m_li = second_factor(p11, exchange(p11))
-    leaf, vup, vlow = leaf_output(pb, xall, u11, alow, cup, clow)
+    cup, clow = parent_assemble(plan, pb, bigm, slab[:, 42], diag, xt)
+    vup, vlow = extend_add(pb, xall, cup, clow)
     sup, slow = exchange((vup, vlow))
-    m_xt = solve(m_u11, m_li, vup, sup)
+    m_xt = solve(m_u11, m_li, (vup, sup))
     core = lax.rem(lax.axis_index("leaf"), 2)
     m_half = gather(lax.dynamic_slice_in_dim(m_xt, core * TB, TB, 0), 2)
+    leaf = leaf_output(xall, u11, alow, m_half)
     merged = merged_output(m_half, exchange(m_half), m_u11, vlow, slow)
     return leaf[None], merged[None]
 

time: 547 us -> 453 us (0.83); the launches traced: 536 us -> 450 us
  waiting for transfers between devices: 144 us -> 95.7 us
  Pallas kernels: 324 us -> 279 us
    all_to_all x2, waiting for transfers between devices: 88.3 us -> 0.01 us  [body(): to_all = lambda x: lax.all_to_all(x, 'front', 0, 0, tiled=True)]
    all_gather x1, waiting for transfers between devices: 40.6 us -> 89 us  [body(): xall = lax.all_gather(xt, 'front')]
    pallas_call x1, Pallas kernels: 32.6 us -> 9.6 us  [parent_assemble(): pl.pallas_call(parent_kernel, out_shape=[f32s(PIV, B), f32s(F - PIV, B)],...]
    pallas_call x4 -> x7, Pallas kernels: 112 us -> 97.4 us  [the longest x1 45.4 us: first_factor(): pl.pallas_call(first_kernel, out_shape=[f32s(PIV, PIV), f32s(PIV, PIV), f...]
    pallas_call x1, Pallas kernels: 15.2 us -> 6.84 us  [leaf_assemble(): pl.pallas_call(leaf_kernel, out_shape=[f32s(PIV, B), f32s(F - PIV, B)], i...]
    ppermute x4, waiting for transfers between devices: 14.8 us -> 6.62 us  [exchange(): return jax.tree.map(lambda v: lax.ppermute(v, 'leaf', route), x)]
  transfers between devices with their start and end apart: 7 -> 7, of which waited for: 3 -> 4; matrix products, arithmetic and copies ran while one was open for 0% -> 0% of each run, Pallas kernels for 34% -> 40%
where the time goes in v2:
time: 453 us; the launch traced here: 450 us
  Pallas kernels  279 us (62%)
  waiting for transfers between devices  95.7 us (21%)
  blocking collectives  30.2 us (7%)
  starting transfers between devices  18.3 us (4%)
  between operations  14.3 us (3%)
  local copies, waits for them, and re-layouts  12.1 us (3%)
    pallas_call x2, Pallas kernels, gather(): pl.pallas_call(gather_kernel, out_shape=jax.ShapeDtypeStruct((NF,) + x.sh...  103 us
    all_gather x1, waiting for transfers between devices, body(): xall = lax.all_gather(xt, 'front')  89 us
    pallas_call x1, Pallas kernels, first_factor(): pl.pallas_call(first_kernel, out_shape=[f32s(PIV, PIV), f32s(PIV, PIV), f...  45.4 us
    pallas_call x1, Pallas kernels, second_factor(): pl.pallas_call(second_kernel, out_shape=[f32s(PIV, PIV), f32s(PIV, TB)],...  34.5 us
    all_to_all x1, blocking collectives, body(): to_all = lambda x: lax.all_to_all(x, 'front', 0, 0, tiled=True)  30.2 us
    pallas_call x2, Pallas kernels, solve(): pl.pallas_call(functools.partial(solve_kernel, len(terms)), out_shape=f32...  16.5 us
    pallas_call x1, Pallas kernels, merged_output(): pl.pallas_call(merged_out_kernel, out_shape=f32s(F, B), in_specs=[VM] * 5...  16.3 us
    pallas_call x1, Pallas kernels, extend_add(): pl.pallas_call(extend_kernel, out_shape=[f32s(PIV, B), f32s(F - PIV, B)],...  15.8 us
  transfers between devices with their start and end apart: 7, of which 4 were waited for; matrix products, arithmetic and copies ran while one was open for 0% of the time, Pallas kernels for 40%

profile of v2, /device:TPU:9, one launch (start us, length us, event | category | flops | bytes accessed | tf_op | source)
XLA Modules:
  0.0 449.7 jit_solution(7683544499095527963)
XLA Ops:
  7.2 1.5 reshape.23.pos
  8.6 11.5 %pack.1 = (bf16[16,27,16,128]{3,2,1,0:T(8,128)(2,1)}, bf16[16,6,128,128]{3,2,1,0:T(8,128)(2,1)}, bf16[16,12,128,128]{3,2,1,0:T(8,128)(2,1)}) custom-call(s32[1536]{0:T(1024)} %reshape.23.pos, s32[13]{0:T(128)} %bitcast.29, bf16[2,24,128,128]{3,2,1,0:T(8,128)(2,1)} %bitcast.23), custom_call_target="tpu_custom_call" | custom-call | tf_op jit(solution)/shard_map/pack/pallas_call | solution.py:132
  20.1 30.2 %all_to_all.15.x = bf16[16,27,16,128]{3,2,1,0:T(8,128)(2,1)} all-to-all(bf16[16,27,16,128]{3,2,1,0:T(8,128)(2,1)} %get-tuple-element.18), channel_id=1, replica_groups=mesh['leaf'=8,'front'=16] {'front'}, dimensions={0} | all-to-all | bytes 3538944 | tf_op jit(solution)/shard_map/all_to_all | solution.py:763
  50.4 5.2 %all-to-all-start.1 = ((bf16[16,6,128,128]{3,2,1,0:T(8,128)(2,1)}), bf16[16,6,128,128]{3,2,1,0:T(8,128)(2,1)S(1)}, u32[]{:S(2)}, u32[]{:S(2)}) async-start(bf16[16,6,128,128]{3,2,1,0:T(8,128)(2,1)} %get-tuple-element.21), calls=%async_computation.1 | async-start | bytes 6291456 | tf_op jit(solution)/shard_map/all_to_all | solution.py:763
  55.6 0.6 copy.13
  56.2 1.8 plan.1
  58.0 3.3 slab.1
  61.3 63.0 %gather1.1 = f32[16,704,128]{2,1,0:T(8,128)} custom-call(f32[704,128]{1,0:T(8,128)} %bitcast.24), custom_call_target="tpu_custom_call" | custom-call | tf_op jit(solution)/shard_map/gather1/pallas_call | solution.py:737
  124.3 1.7 copy-done
  126.0 8.8 %all-to-all-start.2 = ((bf16[16,12,128,128]{3,2,1,0:T(8,128)(2,1)}), bf16[16,12,128,128]{3,2,1,0:T(8,128)(2,1)}, u32[]{:S(2)}, u32[]{:S(2)}) async-start(bf16[16,12,128,128]{3,2,1,0:T(8,128)(2,1)} %get-tuple-element.27), calls=%async_computation.2 | async-start | bytes 12582912 | tf_op jit(solution)/shard_map/all_to_all | solution.py:763
  134.9 6.8 %leafasm.1 = (f32[768,256]{1,0:T(8,128)}, f32[3328,256]{1,0:T(8,128)}) custom-call(s32[96,128]{1,0:T(8,128)} %plan.1, bf16[16,6,128,128]{3,2,1,0:T(8,128)(2,1)} %copy-done, f32[4,128]{1,0:T(4,128)} %bitcast.27, f32[16,44,16,128]{3,2,1,0:T(8,128)} %bitcast.17), custom_call_target="tpu_custom_call" | custom-call | tf_op jit(solution)/shard_map/leafasm/pallas_call | solution.py:298
  141.7 45.4 %first.1 = (f32[768,768]{1,0:T(8,128)}, f32[768,768]{1,0:T(8,128)}, f32[768,128]{1,0:T(8,128)}) custom-call(s32[13]{0:T(128)} %bitcast.31, f32[16,44,16,128]{3,2,1,0:T(8,128)} %bitcast.18, f32[768,256]{1,0:T(8,128)} %get-tuple-element.22.after.refs_0_), custom_call_target="tpu_custom_call" | custom-call | tf_op jit(solution)/shard_map/first/pallas_call | solution.py:459
  187.1 1.6 collective-permute-start
  188.8 4.4 collective-permute-done.other
  193.1 1.5 copy-done.2
  194.6 34.5 %second.1 = (f32[768,768]{1,0:T(8,128)}, f32[768,128]{1,0:T(8,128)}) custom-call(f32[768,768]{1,0:T(8,128)} %get-tuple-element.25.own, f32[768,768]{1,0:T(8,128)} %copy-done.2), custom_call_target="tpu_custom_call" | custom-call | tf_op jit(solution)/shard_map/second/pallas_call | solution.py:476
  229.1 8.1 %solve1.1.after = f32[256,768]{1,0:T(8,128)} custom-call(f32[768,768]{1,0:T(8,128)} %get-tuple-element.23.u.u11, f32[768,128]{1,0:T(8,128)} %get-tuple-element.24.li, f32[768,256]{1,0:T(8,128)} %get-tuple-element.22.after.refs_0_, f32[768,128]{1,0:T(8,128)} %get-tuple-element.26.refs_1_.li, bf16[16,12,128,128]{3,2,1,0:T(8,128)(2,1)} %all-to-all-done.2.refs_2_.x), custom_call_target="tpu_custom_call" | custom-call | tf_op jit(solution)/shard_map/solve1/pallas_call | solution.py:500
  237.3 1.6 slice_bitcast_fusion.extra
  238.9 9.6 %parentasm.1 = (f32[768,256]{1,0:T(8,128)}, f32[3328,256]{1,0:T(8,128)}) custom-call(s32[96,128]{1,0:T(8,128)} %plan.1, s32[13]{0:T(128)} %bitcast.32, bf16[16,12,128,128]{3,2,1,0:T(8,128)(2,1)} %all-to-all-done.2.refs_2_.x, f32[16,16,128]{2,1,0:T(8,128)} %slice_bitcast_fusion.extra, f32[4,128]{1,0:T(4,128)} %bitcast.28, f32[256,768]{1,0:T(8,128)} %solve1.1.after), custom_call_target="tpu_custom_call" | custom-call | tf_op jit(solution)/shard_map/parentasm/pallas_call | solution.py:325
  248.5 89.0 %all-gather.3.cloned.1.call-done = f32[4096,768]{1,0:T(8,128)} async-done(((f32[256,768]{1,0:T(8,128)}), f32[4096,768]{1,0:T(8,128)}) %all-gather.3.cloned.1.call-update) | async-done | bytes 12582928 | tf_op jit(solution)/shard_map/all_gather | solution.py:774
  337.5 15.8 %extend.1 = (f32[768,256]{1,0:T(8,128)}, f32[3328,256]{1,0:T(8,128)}) custom-call(s32[13]{0:T(128)} %bitcast.33, f32[16,256,768]{2,1,0:T(8,128)} %bitcast.20, f32[768,256]{1,0:T(8,128)} %get-tuple-element.30.cup, f32[3328,256]{1,0:T(8,128)} %get-tuple-element.31.clow), custom_call_target="tpu_custom_call" | custom-call | tf_op jit(solution)/shard_map/extend/pallas_call | solution.py:598
  353.3 1.2 collective-permute-start.1
  354.4 2.1 collective-permute-done.1.refs_1_
  356.6 0.9 copy-done.3
  357.4 8.3 %solve2.1 = f32[256,768]{1,0:T(8,128)} custom-call(f32[768,768]{1,0:T(8,128)} %get-tuple-element.29.u.u11, f32[768,128]{1,0:T(8,128)} %get-tuple-element.26.refs_1_.li, f32[768,256]{1,0:T(8,128)} %get-tuple-element.32.refs_0_, f32[768,256]{1,0:T(8,128)} %copy-done.3), custom_call_target="tpu_custom_call" | custom-call | tf_op jit(solution)/shard_map/solve2/pallas_call | solution.py:500
  365.8 1.8 constant_dynamic-slice_fusion.x
  367.5 39.9 %gather2.1.after.xown = f32[16,128,768]{2,1,0:T(8,128)} custom-call(f32[128,768]{1,0:T(8,128)} %constant_dynamic-slice_fusion.x), custom_call_target="tpu_custom_call" | custom-call | tf_op jit(solution)/shard_map/gather2/pallas_call | solution.py:737
  407.5 1.3 collective-permute-start.2
  408.9 14.7 %leafout.1 = f32[4096,256]{1,0:T(8,128)} custom-call(f32[16,256,768]{2,1,0:T(8,128)} %bitcast.21, f32[768,768]{1,0:T(8,128)} %get-tuple-element.23.u.u11, f32[3328,256]{1,0:T(8,128)} %get-tuple-element.28.alow, f32[16,128,768]{2,1,0:T(8,128)} %gather2.1.after.xown), custom_call_target="tpu_custom_call" | custom-call | flops 8000000000 | bytes 30000000 | tf_op jit(solution)/shard_map/leafout/pallas_call | solution.py:613
  423.5 0.1 collective-permute-done.3.low1
  423.7 2.7 copy-done.1
  426.3 16.3 %mergedout.1 = f32[4096,256]{1,0:T(8,128)} custom-call(f32[16,128,768]{2,1,0:T(8,128)} %gather2.1.after.xown, f32[16,128,768]{2,1,0:T(8,128)} %copy-done.1, f32[768,768]{1,0:T(8,128)} %get-tuple-element.29.u.u11, f32[3328,256]{1,0:T(8,128)} %get-tuple-element.33.low0, f32[3328,256]{1,0:T(8,128)} %collective-permute-done.3.low1), custom_call_target="tpu_custom_call" | custom-call | tf_op jit(solution)/shard_map/mergedout/pallas_call | solution.py:642
  (12 shorter events, 0.2 us)
Async XLA Ops:
  50.4 5.2 %copy-start.4 = (s32[2,1,16,2,24]{4,3,2,1,0:T(2,128)S(1)}, s32[2,1,16,2,24]{4,3,2,1,0:T(2,128)}, u32[]{:S(2)}) copy-start(s32[2,1,16,2,24]{4,3,2,1,0:T(2,128)} %param.5) | copy-start | bytes 18436
  50.4 73.9 %all-to-all-start.1 = ((bf16[16,6,128,128]{3,2,1,0:T(8,128)(2,1)}), bf16[16,6,128,128]{3,2,1,0:T(8,128)(2,1)S(1)}, u32[]{:S(2)}, u32[]{:S(2)}) async-start(bf16[16,6,128,128]{3,2,1,0:T(8,128)(2,1)} %get-tuple-element.21), calls=%async_computation.1 | async-start | bytes 6291456 | tf_op jit(solution)/shard_map/all_to_all | solution.py:763
  124.3 1.7 copy-start
  126.0 103.2 %all-to-all-start.2 = ((bf16[16,12,128,128]{3,2,1,0:T(8,128)(2,1)}), bf16[16,12,128,128]{3,2,1,0:T(8,128)(2,1)}, u32[]{:S(2)}, u32[]{:S(2)}) async-start(bf16[16,12,128,128]{3,2,1,0:T(8,128)(2,1)} %get-tuple-element.27), calls=%async_computation.2 | async-start | bytes 12582912 | tf_op jit(solution)/shard_map/all_to_all | solution.py:763
  134.8 202.7 %all-gather.3.cloned.1.call-start = ((), (), s32[]{:S(2)}) async-start(), calls=%async_computation.3 | async-start | bytes 13369344 | tf_op jit(solution)/shard_map/all_gather | solution.py:774
  187.1 6.0 %collective-permute-start = (f32[768,768]{1,0:T(8,128)}, f32[768,768]{1,0:T(8,128)S(1)}, u32[]{:S(2)}, u32[]{:S(2)}) collective-permute-start(f32[768,768]{1,0:T(8,128)} %get-tuple-element.25.own), channel_id=1, source_target_pairs={{0,16},{16,0},{32,48},{48,32},{64,80},{80,64},{96,112},{112,96},{1... | collective-permute-start | bytes 7077896 | tf_op jit(solution)/shard_map/ppermute | solution.py:754
  193.1 1.5 copy-start.2
  353.3 3.3 collective-permute-start.1
  356.6 0.9 copy-start.3
  407.5 16.2 %collective-permute-start.2 = (f32[16,128,768]{2,1,0:T(8,128)}, f32[16,128,768]{2,1,0:T(8,128)S(1)}, u32[]{:S(2)}, u32[]{:S(2)}) collective-permute-start(f32[16,128,768]{2,1,0:T(8,128)} %gather2.1.after.xown), channel_id=1, source_target_pairs={{0,16},{16,0},{32,48},{48,32},{64,80},{80,64},{96,112},{112,96},{1... | collective-permute-start | bytes 18874376 | tf_op jit(solution)/shard_map/ppermute | solution.py:754
  408.8 14.9 %collective-permute-start.3 = (f32[3328,256]{1,0:T(8,128)}, f32[3328,256]{1,0:T(8,128)}, u32[]{:S(2)}, u32[]{:S(2)}) collective-permute-start(f32[3328,256]{1,0:T(8,128)} %get-tuple-element.33.low0), channel_id=1, source_target_pairs={{0,16},{16,0},{32,48},{48,32},{64,80},{80,64},{96,112},{112,96},{1... | collective-permute-start | bytes 10223624 | tf_op jit(solution)/shard_map/ppermute | solution.py:754
  423.7 2.7 copy-start.1
Sparse Core Ops, SparseCore 0:
  237.4 100.0 all-gather.2

commit v3 on v2

--- a/solution.py
+++ b/solution.py
@@ -771,7 +771,7 @@
     u11, p11, li = first_factor(pb, slab, aup)
     m_u11, m_li = second_factor(p11, exchange(p11))
     xt = solve(u11, li, (aup,), (m_li, bigm))
-    xall = lax.all_gather(xt, "front")
+    xall = gather(xt, 3)
     cup, clow = parent_assemble(plan, pb, bigm, slab[:, 42], diag, xt)
     vup, vlow = extend_add(pb, xall, cup, clow)
     sup, slow = exchange((vup, vlow))

time: 453 us -> 431 us (0.951)
  waiting for transfers between devices: 95.7 us -> 5.41 us
  Pallas kernels: 279 us -> 358 us
  between operations: 14.3 us -> 0.88 us
    all_gather x1 -> x0, waiting for transfers between devices: 89 us -> none  [body(): xall = lax.all_gather(xt, 'front')]
    pallas_call x2 -> x3, Pallas kernels: 103 us -> 181 us  [gather(): pl.pallas_call(gather_kernel, out_shape=jax.ShapeDtypeStruct((NF,) + x.sh...]
  transfers between devices with their start and end apart: 7 -> 6, of which waited for: 4 -> 3; matrix products, arithmetic and copies ran while one was open for 0% -> 1% of each run, Pallas kernels for 40% -> 40%
where the time goes in v3:
time: 431 us; the launch traced here: 426 us
  Pallas kernels  358 us (83%)
  blocking collectives  30.2 us (7%)
  starting transfers between devices  19.1 us (4%)
  local copies, waits for them, and re-layouts  12.1 us (3%)
  waiting for transfers between devices  5.41 us (1%)
    pallas_call x3, Pallas kernels, gather(): pl.pallas_call(gather_kernel, out_shape=jax.ShapeDtypeStruct((NF,) + x.sh...  181 us
    pallas_call x1, Pallas kernels, first_factor(): pl.pallas_call(first_kernel, out_shape=[f32s(PIV, PIV), f32s(PIV, PIV), f...  45.4 us
    pallas_call x1, Pallas kernels, second_factor(): pl.pallas_call(second_kernel, out_shape=[f32s(PIV, PIV), f32s(PIV, TB)],...  34.8 us
    all_to_all x1, blocking collectives, body(): to_all = lambda x: lax.all_to_all(x, 'front', 0, 0, tiled=True)  30.2 us
    pallas_call x2, Pallas kernels, solve(): pl.pallas_call(functools.partial(solve_kernel, len(terms)), out_shape=f32...  16.4 us
    pallas_call x1, Pallas kernels, merged_output(): pl.pallas_call(merged_out_kernel, out_shape=f32s(F, B), in_specs=[VM] * 5...  16.3 us
    pallas_call x1, Pallas kernels, extend_add(): pl.pallas_call(extend_kernel, out_shape=[f32s(PIV, B), f32s(F - PIV, B)],...  15.8 us
    pallas_call x1, Pallas kernels, leaf_output(): pl.pallas_call(leaf_out_kernel, out_shape=f32s(F, B), in_specs=[VM] * 3 +...  14.7 us
  transfers between devices with their start and end apart: 6, of which 3 were waited for; matrix products, arithmetic and copies ran while one was open for 1% of the time, Pallas kernels for 40%

profile of v3, /device:TPU:9, one launch (start us, length us, event | category | flops | bytes accessed | tf_op | source)
XLA Modules:
  0.0 426.0 jit_solution(8104966030727081525)
XLA Ops:
  0.6 1.4 reshape.23.pos
  2.1 11.5 %pack.1 = (bf16[16,27,16,128]{3,2,1,0:T(8,128)(2,1)}, bf16[16,6,128,128]{3,2,1,0:T(8,128)(2,1)}, bf16[16,12,128,128]{3,2,1,0:T(8,128)(2,1)}) custom-call(s32[1536]{0:T(1024)} %reshape.23.pos, s32[13]{0:T(128)} %bitcast.26, bf16[2,24,128,128]{3,2,1,0:T(8,128)(2,1)} %bitcast.20), custom_call_target="tpu_custom_call" | custom-call | tf_op jit(solution)/shard_map/pack/pallas_call | solution.py:132
  13.6 30.2 %all_to_all.15.x = bf16[16,27,16,128]{3,2,1,0:T(8,128)(2,1)} all-to-all(bf16[16,27,16,128]{3,2,1,0:T(8,128)(2,1)} %get-tuple-element.18), channel_id=1, replica_groups=mesh['leaf'=8,'front'=16] {'front'}, dimensions={0} | all-to-all | bytes 3538944 | tf_op jit(solution)/shard_map/all_to_all | solution.py:763
  43.8 5.2 %all-to-all-start.1 = ((bf16[16,6,128,128]{3,2,1,0:T(8,128)(2,1)}), bf16[16,6,128,128]{3,2,1,0:T(8,128)(2,1)S(1)}, u32[]{:S(2)}, u32[]{:S(2)}) async-start(bf16[16,6,128,128]{3,2,1,0:T(8,128)(2,1)} %get-tuple-element.21), calls=%async_computation.1 | async-start | bytes 6291456 | tf_op jit(solution)/shard_map/all_to_all | solution.py:763
  48.9 0.6 copy.13
  49.6 1.8 plan.1
  51.3 3.4 slab.1
  54.7 63.1 %gather1.1 = f32[16,704,128]{2,1,0:T(8,128)} custom-call(f32[704,128]{1,0:T(8,128)} %bitcast.21), custom_call_target="tpu_custom_call" | custom-call | tf_op jit(solution)/shard_map/gather1/pallas_call | solution.py:737
  117.8 1.7 copy-done
  119.4 8.9 %all-to-all-start.2 = ((bf16[16,12,128,128]{3,2,1,0:T(8,128)(2,1)}), bf16[16,12,128,128]{3,2,1,0:T(8,128)(2,1)}, u32[]{:S(2)}, u32[]{:S(2)}) async-start(bf16[16,12,128,128]{3,2,1,0:T(8,128)(2,1)} %get-tuple-element.27), calls=%async_computation.2 | async-start | bytes 12582912 | tf_op jit(solution)/shard_map/all_to_all | solution.py:763
  128.3 7.4 %leafasm.1 = (f32[768,256]{1,0:T(8,128)}, f32[3328,256]{1,0:T(8,128)}) custom-call(s32[96,128]{1,0:T(8,128)} %plan.1, bf16[16,6,128,128]{3,2,1,0:T(8,128)(2,1)} %copy-done, f32[4,128]{1,0:T(4,128)} %bitcast.24, f32[16,44,16,128]{3,2,1,0:T(8,128)} %bitcast.16), custom_call_target="tpu_custom_call" | custom-call | tf_op jit(solution)/shard_map/leafasm/pallas_call | solution.py:298
  135.8 45.4 %first.1 = (f32[768,768]{1,0:T(8,128)}, f32[768,768]{1,0:T(8,128)}, f32[768,128]{1,0:T(8,128)}) custom-call(s32[13]{0:T(128)} %bitcast.28, f32[16,44,16,128]{3,2,1,0:T(8,128)} %bitcast.17, f32[768,256]{1,0:T(8,128)} %get-tuple-element.22.after.refs_0_), custom_call_target="tpu_custom_call" | custom-call | tf_op jit(solution)/shard_map/first/pallas_call | solution.py:459
  181.1 0.2 collective-permute-start
  181.3 1.6 slice_bitcast_fusion.extra
  182.8 3.2 collective-permute-done.other
  186.0 1.5 copy-done.2
  187.5 34.8 %second.1 = (f32[768,768]{1,0:T(8,128)}, f32[768,128]{1,0:T(8,128)}) custom-call(f32[768,768]{1,0:T(8,128)} %get-tuple-element.25.own, f32[768,768]{1,0:T(8,128)} %copy-done.2), custom_call_target="tpu_custom_call" | custom-call | tf_op jit(solution)/shard_map/second/pallas_call | solution.py:476
  222.3 8.1 %solve1.1.x.after = f32[256,768]{1,0:T(8,128)} custom-call(f32[768,768]{1,0:T(8,128)} %get-tuple-element.23.u.u11, f32[768,128]{1,0:T(8,128)} %get-tuple-element.24.li, f32[768,256]{1,0:T(8,128)} %get-tuple-element.22.after.refs_0_, f32[768,128]{1,0:T(8,128)} %get-tuple-element.26.refs_1_.li, bf16[16,12,128,128]{3,2,1,0:T(8,128)(2,1)} %all-to-all-done.2.refs_2_.x), custom_call_target="tpu_custom_call" | custom-call | tf_op jit(solution)/shard_map/solve1/pallas_call | solution.py:500
  230.3 78.4 %gather3.1.xall = f32[16,256,768]{2,1,0:T(8,128)} custom-call(f32[256,768]{1,0:T(8,128)} %solve1.1.x.after), custom_call_target="tpu_custom_call" | custom-call | tf_op jit(solution)/shard_map/gather3/pallas_call | solution.py:737
  308.7 10.3 %parentasm.1 = (f32[768,256]{1,0:T(8,128)}, f32[3328,256]{1,0:T(8,128)}) custom-call(s32[96,128]{1,0:T(8,128)} %plan.1, s32[13]{0:T(128)} %bitcast.29, bf16[16,12,128,128]{3,2,1,0:T(8,128)(2,1)} %all-to-all-done.2.refs_2_.x, f32[16,16,128]{2,1,0:T(8,128)} %slice_bitcast_fusion.extra, f32[4,128]{1,0:T(4,128)} %bitcast.25, f32[256,768]{1,0:T(8,128)} %solve1.1.x.after), custom_call_target="tpu_custom_call" | custom-call | tf_op jit(solution)/shard_map/parentasm/pallas_call | solution.py:325
  319.1 15.8 %extend.1 = (f32[768,256]{1,0:T(8,128)}, f32[3328,256]{1,0:T(8,128)}) custom-call(s32[13]{0:T(128)} %bitcast.30, f32[16,256,768]{2,1,0:T(8,128)} %gather3.1.xall, f32[768,256]{1,0:T(8,128)} %get-tuple-element.30.cup, f32[3328,256]{1,0:T(8,128)} %get-tuple-element.31.clow), custom_call_target="tpu_custom_call" | custom-call | tf_op jit(solution)/shard_map/extend/pallas_call | solution.py:598
  334.8 3.5 collective-permute-start.1
  338.4 2.1 collective-permute-done.1.refs_1_
  340.5 0.9 copy-done.3
  341.4 8.3 %solve2.1 = f32[256,768]{1,0:T(8,128)} custom-call(f32[768,768]{1,0:T(8,128)} %get-tuple-element.29.u.u11, f32[768,128]{1,0:T(8,128)} %get-tuple-element.26.refs_1_.li, f32[768,256]{1,0:T(8,128)} %get-tuple-element.32.refs_0_, f32[768,256]{1,0:T(8,128)} %copy-done.3), custom_call_target="tpu_custom_call" | custom-call | tf_op jit(solution)/shard_map/solve2/pallas_call | solution.py:500
  349.7 1.8 constant_dynamic-slice_fusion.x
  351.5 39.3 %gather2.1.after.xown = f32[16,128,768]{2,1,0:T(8,128)} custom-call(f32[128,768]{1,0:T(8,128)} %constant_dynamic-slice_fusion.x), custom_call_target="tpu_custom_call" | custom-call | tf_op jit(solution)/shard_map/gather2/pallas_call | solution.py:737
  390.7 1.3 collective-permute-start.2
  392.1 14.7 %leafout.1 = f32[4096,256]{1,0:T(8,128)} custom-call(f32[16,256,768]{2,1,0:T(8,128)} %gather3.1.xall, f32[768,768]{1,0:T(8,128)} %get-tuple-element.23.u.u11, f32[3328,256]{1,0:T(8,128)} %get-tuple-element.28.alow, f32[16,128,768]{2,1,0:T(8,128)} %gather2.1.after.xown), custom_call_target="tpu_custom_call" | custom-call | flops 8000000000 | bytes 30000000 | tf_op jit(solution)/shard_map/leafout/pallas_call | solution.py:613
  406.8 0.1 collective-permute-done.3.low1
  406.9 2.7 copy-done.1
  409.6 16.3 %mergedout.1 = f32[4096,256]{1,0:T(8,128)} custom-call(f32[16,128,768]{2,1,0:T(8,128)} %gather2.1.after.xown, f32[16,128,768]{2,1,0:T(8,128)} %copy-done.1, f32[768,768]{1,0:T(8,128)} %get-tuple-element.29.u.u11, f32[3328,256]{1,0:T(8,128)} %get-tuple-element.33.low0, f32[3328,256]{1,0:T(8,128)} %collective-permute-done.3.low1), custom_call_target="tpu_custom_call" | custom-call | tf_op jit(solution)/shard_map/mergedout/pallas_call | solution.py:642
  (10 shorter events, 0.1 us)
Async XLA Ops:
  43.8 5.2 %copy-start.4 = (s32[2,1,16,2,24]{4,3,2,1,0:T(2,128)S(1)}, s32[2,1,16,2,24]{4,3,2,1,0:T(2,128)}, u32[]{:S(2)}) copy-start(s32[2,1,16,2,24]{4,3,2,1,0:T(2,128)} %param.5) | copy-start | bytes 18436
  43.8 74.0 %all-to-all-start.1 = ((bf16[16,6,128,128]{3,2,1,0:T(8,128)(2,1)}), bf16[16,6,128,128]{3,2,1,0:T(8,128)(2,1)S(1)}, u32[]{:S(2)}, u32[]{:S(2)}) async-start(bf16[16,6,128,128]{3,2,1,0:T(8,128)(2,1)} %get-tuple-element.21), calls=%async_computation.1 | async-start | bytes 6291456 | tf_op jit(solution)/shard_map/all_to_all | solution.py:763
  117.8 1.7 copy-start
  119.4 102.8 %all-to-all-start.2 = ((bf16[16,12,128,128]{3,2,1,0:T(8,128)(2,1)}), bf16[16,12,128,128]{3,2,1,0:T(8,128)(2,1)}, u32[]{:S(2)}, u32[]{:S(2)}) async-start(bf16[16,12,128,128]{3,2,1,0:T(8,128)(2,1)} %get-tuple-element.27), calls=%async_computation.2 | async-start | bytes 12582912 | tf_op jit(solution)/shard_map/all_to_all | solution.py:763
  181.1 4.9 %collective-permute-start = (f32[768,768]{1,0:T(8,128)}, f32[768,768]{1,0:T(8,128)S(1)}, u32[]{:S(2)}, u32[]{:S(2)}) collective-permute-start(f32[768,768]{1,0:T(8,128)} %get-tuple-element.25.own), channel_id=1, source_target_pairs={{0,16},{16,0},{32,48},{48,32},{64,80},{80,64},{96,112},{112,96},{1... | collective-permute-start | bytes 7077896 | tf_op jit(solution)/shard_map/ppermute | solution.py:754
  186.0 1.5 copy-start.2
  334.8 5.7 %collective-permute-start.1 = (f32[768,256]{1,0:T(8,128)}, f32[768,256]{1,0:T(8,128)S(1)}, u32[]{:S(2)}, u32[]{:S(2)}) collective-permute-start(f32[768,256]{1,0:T(8,128)} %get-tuple-element.32.refs_0_), channel_id=1, source_target_pairs={{0,16},{16,0},{32,48},{48,32},{64,80},{80,64},{96,112},{112,96},{1... | collective-permute-start | bytes 2359304 | tf_op jit(solution)/shard_map/ppermute | solution.py:754
  340.5 0.9 copy-start.3
  390.7 16.2 %collective-permute-start.2 = (f32[16,128,768]{2,1,0:T(8,128)}, f32[16,128,768]{2,1,0:T(8,128)S(1)}, u32[]{:S(2)}, u32[]{:S(2)}) collective-permute-start(f32[16,128,768]{2,1,0:T(8,128)} %gather2.1.after.xown), channel_id=1, source_target_pairs={{0,16},{16,0},{32,48},{48,32},{64,80},{80,64},{96,112},{112,96},{1... | collective-permute-start | bytes 18874376 | tf_op jit(solution)/shard_map/ppermute | solution.py:754
  392.0 14.9 %collective-permute-start.3 = (f32[3328,256]{1,0:T(8,128)}, f32[3328,256]{1,0:T(8,128)}, u32[]{:S(2)}, u32[]{:S(2)}) collective-permute-start(f32[3328,256]{1,0:T(8,128)} %get-tuple-element.33.low0), channel_id=1, source_target_pairs={{0,16},{16,0},{32,48},{48,32},{64,80},{80,64},{96,112},{112,96},{1... | collective-permute-start | bytes 10223624 | tf_op jit(solution)/shard_map/ppermute | solution.py:754
  406.9 2.7 copy-start.1
